TPU v7x, 32 devices: a whole 2x2x4 slice. The times are simulated.
32 devices in a mesh: px: 8 (over y, x, core), py: 4 (over z).
Axes of the slice: x: 2, y: 2, z: 4, core: 2. Of those that a mesh axis runs over, the one named last changes fastest.
Arguments:
- density: float32 [512, 512, 256], P('px', 'py'), may hold values from -6 to 6
- external: float32 [512, 512, 256], P('px', 'py'), may hold values from -6 to 6
- orbitals: float32 [64, 8, 24, 576], P(('px', 'py')), may hold values from -6 to 6
- anchors: int32 [64, 3], P(('px', 'py')), may hold values from 0 to 511, as said below
- weights: int32 [64], P(('px', 'py')), may hold values from -1 to 1, as said below
- degrees: int32 [64], P(('px', 'py')), may hold values from 4 to 24
Outputs:
- hartree_field: float32 [512, 512, 256], P('px', 'py')
- filtered: float32 [64, 8, 24, 576], P(('px', 'py'))
- new_density: float32 [512, 512, 256], P('px', 'py')
Inputs may be any that keep to these rules, and one draw needn't show every extreme that they name: `anchors`: fragment f lies on device f // 2 of the joined px, py axes; its anchor's first two coordinates lie in that device's block of the grid, its third coordinate is at most 232. `weights`: each weight is -1 or +1.
All inputs are finite; a program needn't handle non-finite values.
Results may differ from a plain program's by a relative error of at most 0.0003.
Values sent between devices are 32-bit elements; how exact they have to be, the bound alone decides.
A program may use at most 128 MiB of HBM per device.

v0:
```python
import jax
import jax.numpy as jnp
from jax import lax
from jax.sharding import PartitionSpec as P

NX = 512
NY = 512
NZ = 256


screening = 0.002
window_gap = 0.1
kinetic_top = 6.0
highest = lax.Precision.HIGHEST


def shifted(x, axis, by):
    peers = lax.axis_size(axis)
    pairs = [(i, i + by) for i in range(peers) if 0 <= i + by < peers]
    return lax.ppermute(x, axis, pairs)


def partner(x, axis, bit):
    return lax.ppermute(x, axis, [(i, i ^ 1 << bit) for i in range(lax.axis_size(axis))])


def sine_table(length):
    indices = jnp.arange(1, length + 1, dtype=jnp.int32)
    product = indices[:, None] * indices[None, :] % (2 * length + 2)
    angle = product.astype(jnp.float32) * (jnp.pi / (length + 1))
    return jnp.sin(angle) * jnp.sqrt(2.0 / (length + 1))


def eigen_values(start, count, length):
    wave = (start + jnp.arange(count, dtype=jnp.int32) + 1).astype(jnp.float32)
    return 2.0 - 2.0 * jnp.cos(wave * (jnp.pi / (length + 1)))


def along_first(field, table):
    return jnp.einsum("abc,ak->kbc", field, table, precision=highest)


def along_second(field, table):
    return jnp.einsum("abc,bk->akc", field, table, precision=highest)


def along_third(field, table):
    return jnp.einsum("abc,ck->abk", field, table, precision=highest)


def neighbours(field):
    frag_edge = field.shape[-2]
    zero_row = jnp.zeros_like(field[..., :1, :])
    total = jnp.concatenate([field[..., 1:, :], zero_row], -2) + jnp.concatenate(
        [zero_row, field[..., :-1, :]], -2
    )
    zero_cols = jnp.zeros_like(field[..., :frag_edge])
    total = (
        total
        + jnp.concatenate([field[..., frag_edge:], zero_cols], -1)
        + jnp.concatenate([zero_cols, field[..., :-frag_edge]], -1)
    )
    zero_one = jnp.zeros_like(field[..., :1])
    inner = jnp.arange(field.shape[-1], dtype=jnp.int32) % frag_edge
    forward = jnp.concatenate([field[..., 1:], zero_one], -1)
    backward = jnp.concatenate([zero_one, field[..., :-1]], -1)
    total = (
        total
        + jnp.where(inner == frag_edge - 1, 0.0, forward)
        + jnp.where(inner == 0, 0.0, backward)
    )
    return total


def chebyshev(orbital_set, box, degree_set, steps):
    low = jnp.min(box, axis=(1, 2)) + window_gap
    high = jnp.max(box, axis=(1, 2)) + kinetic_top
    centre = (0.5 * (high + low))[:, None, None, None]
    half_width = (0.5 * (high - low))[:, None, None, None]
    potential = box[:, None]

    def advance(counter, state):
        before, current = state
        image = 3.0 * current - 0.5 * neighbours(current) + potential * current
        scaled = (image - centre * current) / half_width
        following = jnp.where(counter == 0, scaled, 2.0 * scaled - before)
        live = (counter < degree_set)[:, None, None, None]
        return (jnp.where(live, current, before), jnp.where(live, following, current))

    before, current = lax.fori_loop(0, steps, advance, (orbital_set, orbital_set))
    cells = orbital_set.shape[2] ** 3
    squares = jnp.sum(current * current, axis=(2, 3), keepdims=True)
    return current * jnp.sqrt(cells / (squares + 1e-06))


def filter_set(orbital_set, box_set, degree_set):

    def filter_one(parcel):
        orbital_one, box_one, degree_one = parcel
        return chebyshev(orbital_one[None], box_one[None], degree_one[None], degree_one)[0]

    return lax.map(filter_one, (orbital_set, box_set, degree_set))


def pair_assignment(lower_degrees, upper_degrees):
    count = lower_degrees.shape[0]
    joined = jnp.concatenate([lower_degrees, upper_degrees])
    order_key = joined * (2 * count) + (2 * count - 1 - jnp.arange(2 * count, dtype=jnp.int32))
    ordering = jnp.argsort(-order_key)
    assigned = jnp.zeros((2 * count,), jnp.int32)
    totals = jnp.zeros((2,), jnp.int32)
    filled = jnp.zeros((2,), jnp.int32)
    for ranked in range(2 * count):
        picked = ordering[ranked]
        picked_degree = joined[picked]
        chosen = jnp.where(
            filled[0] >= count,
            1,
            jnp.where(filled[1] >= count, 0, jnp.where(totals[1] < totals[0], 1, 0)),
        ).astype(jnp.int32)
        assigned = assigned.at[picked].set(chosen)
        totals = totals.at[chosen].add(picked_degree)
        filled = filled.at[chosen].add(1)
    return assigned


def solve_rows(density):
    row_place = lax.axis_index("px")
    col_place = lax.axis_index("py")
    spectrum = along_third(density, sine_table(density.shape[2]))
    spectrum = lax.all_to_all(spectrum, "px", split_axis=2, concat_axis=0, tiled=True)
    table_x = sine_table(spectrum.shape[0])
    spectrum = along_first(spectrum, table_x)
    spectrum = lax.all_to_all(spectrum, "py", split_axis=0, concat_axis=1, tiled=True)
    size_x, size_y, size_z = spectrum.shape
    table_y = sine_table(size_y)
    spectrum = along_second(spectrum, table_y)
    divisor = (
        eigen_values(col_place * size_x, size_x, NX)[:, None, None]
        + eigen_values(0, size_y, NY)[None, :, None]
        + eigen_values(row_place * size_z, size_z, NZ)[None, None, :]
        + screening
    )
    spectrum = along_second(spectrum / divisor, table_y)
    spectrum = lax.all_to_all(spectrum, "py", split_axis=1, concat_axis=0, tiled=True)
    spectrum = along_first(spectrum, table_x)
    spectrum = lax.all_to_all(spectrum, "px", split_axis=0, concat_axis=2, tiled=True)
    return along_third(spectrum, sine_table(NZ))


def body(density, external, orbitals, anchors, weights, degrees):
    row_count, col_count, depth = density.shape
    frag_count, orbital_count, frag_edge, merged = orbitals.shape
    row_place = lax.axis_index("px")
    col_place = lax.axis_index("py")
    hops_rows = -(-frag_edge // row_count)
    hartree_field = solve_rows(density)
    potential = hartree_field + external
    row_tail = jnp.zeros((frag_edge, col_count, depth), jnp.float32)
    for crossing in range(hops_rows):
        joined_rows = jnp.concatenate([potential, row_tail], 0)
        row_tail = shifted(joined_rows[:frag_edge], "px", -1)
    widened = jnp.concatenate([potential, row_tail], 0)
    col_tail = jnp.zeros((row_count + frag_edge, frag_edge, depth), jnp.float32)
    joined_cols = jnp.concatenate([widened, col_tail], 1)
    col_tail = shifted(joined_cols[:, :frag_edge], "py", -1)
    widened = jnp.concatenate([widened, col_tail], 1)
    local = jnp.stack(
        [
            anchors[:, 0] - row_place * row_count,
            anchors[:, 1] - col_place * col_count,
            anchors[:, 2],
        ],
        1,
    )

    def cut_box(corner):
        return lax.dynamic_slice(
            widened, (corner[0], corner[1], corner[2]), (frag_edge, frag_edge, frag_edge)
        ).reshape(frag_edge, merged)

    boxes = jax.vmap(cut_box)(local)
    partner_degrees = partner(degrees, "py", 0)
    is_lower = col_place % 2 == 0
    lower_degrees = jnp.where(is_lower, degrees, partner_degrees)
    upper_degrees = jnp.where(is_lower, partner_degrees, degrees)
    assigned = pair_assignment(lower_degrees, upper_degrees)
    my_side = jnp.where(is_lower, 0, 1)
    own_side = jnp.where(is_lower, assigned[:frag_count], assigned[frag_count:])
    partner_side = jnp.where(is_lower, assigned[frag_count:], assigned[:frag_count])
    moving = own_side != my_side
    guests = partner_side == my_side
    parcel = jnp.concatenate([orbitals, boxes[:, None]], 1)
    parcel = jnp.where(moving[:, None, None, None], parcel, 0.0)
    arrived = partner(parcel, "py", 0)
    guest_done = filter_set(
        arrived[:, :orbital_count], arrived[:, orbital_count], jnp.where(guests, partner_degrees, 0)
    )
    guest_done = jnp.where(guests[:, None, None, None], guest_done, 0.0)
    returned = partner(guest_done, "py", 0)
    own_done = filter_set(orbitals, boxes, jnp.where(moving, 0, degrees))
    filtered = jnp.where(moving[:, None, None, None], returned, own_done)
    weight_scale = weights.astype(jnp.float32) / orbital_count
    contribution = weight_scale[:, None, None] * jnp.sum(filtered * filtered, axis=1)

    def place(counter, total):
        corner = (local[counter, 0], local[counter, 1], local[counter, 2])
        block = contribution[counter].reshape(frag_edge, frag_edge, frag_edge)
        current = lax.dynamic_slice(total, corner, (frag_edge, frag_edge, frag_edge))
        return lax.dynamic_update_slice(total, current + block, corner)

    patched = jnp.zeros((row_count + frag_edge, col_count + frag_edge, depth), jnp.float32)
    patched = lax.fori_loop(0, frag_count, place, patched)
    spill_cols = shifted(patched[:, col_count:], "py", 1)
    patched = jnp.concatenate([patched[:, :col_count], jnp.zeros_like(spill_cols)], 1)
    patched = patched.at[:, :frag_edge].add(spill_cols)
    patched = patched[:, :col_count]
    for crossing in range(hops_rows):
        spill_rows = shifted(patched[row_count:], "px", 1)
        patched = jnp.concatenate([patched[:row_count], jnp.zeros_like(spill_rows)], 0)
        patched = patched.at[:frag_edge].add(spill_rows)
    new_density = patched[:row_count]
    return (hartree_field, filtered, new_density)


def solution(mesh):
    placed = (
        P("px", "py", None),
        P("px", "py", None),
        P(("px", "py"), None, None, None),
        P(("px", "py"), None),
        P(("px", "py")),
        P(("px", "py")),
    )
    return jax.shard_map(
        body,
        mesh=mesh,
        in_specs=placed,
        out_specs=(P("px", "py", None), P(("px", "py"), None, None, None), P("px", "py", None)),
        check_vma=False,
    )
```

profile of v0, /device:TPU:18, one launch (start us, length us, event | category | flops | bytes accessed | tf_op | source)
XLA Modules:
  0.0 1161.4 jit_solution(13378673558418302033)
XLA Ops:
  0.6 19.9 %convolution_bitcast_fusion = f32[64,128,256]{1,2,0:T(8,128)S(1)} fusion(f32[64,128,256]{2,1,0:T(8,128)} %param.40, s32[256]{0:T(256)S(1)} %iota_add_fusion.1), kind=kOutput, calls=%fused_computation.48 | convolution fusion | flops 6443106304 | bytes 16778240 | tf_op jit(solution)/shard_map/abc,ck->abk/dot_general | solution.py:48
  20.5 8.3 copy.36
  34.3 92.5 %all-to-all-done = f32[64,128,256]{1,0,2:T(8,128)} async-done(((f32[64,128,256]{1,0,2:T(8,128)}), f32[64,128,256]{1,0,2:T(8,128)}, u32[]{:S(2)}, u32[]{:S(2)}) %all-to-all-start) | async-done | bytes 8388640 | tf_op jit(solution)/shard_map/all_to_all | solution.py:131
  131.0 18.8 %fusion.32 = f32[512,128,32]{1,0,2:T(8,128)S(1)} fusion(f32[512,128,32]{1,0,2:T(8,128)S(1)} %bitcast.140, s32[512]{0:T(512)S(1)} %iota_add_fusion), kind=kOutput, calls=%fused_computation.68 | convolution fusion | flops 12887523328 | bytes 16779264 | tf_op jit(solution)/shard_map/abc,ak->kbc/dot_general | solution.py:40
  149.8 8.3 copy.38
  164.0 180.2 %all-to-all-done.1 = f32[512,128,32]{1,2,0:T(8,128)} async-done(((f32[512,128,32]{1,2,0:T(8,128)}), f32[512,128,32]{1,2,0:T(8,128)}, u32[]{:S(2)}, u32[]{:S(2)}) %all-to-all-start.1) | async-done | bytes 8388640 | tf_op jit(solution)/shard_map/all_to_all | solution.py:134
  344.2 10.3 copy.54
  354.5 21.7 %fusion.30 = f32[512,128,32]{1,0,2:T(8,128)S(1)} fusion(f32[128,512,32]{0,1,2:T(8,128)} %bitcast.141, s32[512]{0:T(512)S(1)} %iota_add_fusion), kind=kOutput, calls=%fused_computation.67 | convolution fusion | flops 12887523328 | bytes 16779264 | tf_op jit(solution)/shard_map/abc,bk->akc/dot_general | solution.py:44
  376.2 19.4 %fusion.16 = f32[128,512,32]{0,1,2:T(8,128)S(1)} fusion(f32[512,128,32]{1,0,2:T(8,128)S(1)} %fusion.30, f32[32]{0:T(128)S(1)} %multiply_subtract_fusion.1, f32[128,512]{0,1:T(8,128)S(1)} %broadcast_add_fusion, s32[512]{0:T(512)S(1)} %iota_add_fusion), kind=kOutput, calls=%fused_computation.49 | convolution fusion | flops 12893814784 | bytes 17041536 | tf_op jit(solution)/shard_map/abc,bk->akc/dot_general | solution.py:44
  400.7 187.9 %all_to_all.72 = f32[128,512,32]{0,2,1:T(8,128)} all-to-all(f32[128,512,32]{0,2,1:T(8,128)S(1)} %copy.42), channel_id=1, replica_groups=mesh['px'=8,'py'=4] {'py'}, dimensions={1} | all-to-all | bytes 16777216 | tf_op jit(solution)/shard_map/all_to_all | solution.py:145
  588.7 9.9 copy.43
  598.6 22.2 %fusion.27 = f32[512,128,32]{1,0,2:T(8,128)S(1)} fusion(f32[512,128,32]{1,0,2:T(8,128)} %bitcast.139, s32[512]{0:T(512)S(1)} %iota_add_fusion), kind=kOutput, calls=%fused_computation.66 | convolution fusion | flops 12887523328 | bytes 16779264 | tf_op jit(solution)/shard_map/abc,ak->kbc/dot_general | solution.py:40
  625.6 95.8 %all_to_all.73 = f32[512,128,32]{1,2,0:T(8,128)S(1)} all-to-all(f32[512,128,32]{1,2,0:T(8,128)S(1)} %copy.44), channel_id=1, replica_groups=mesh['px'=8,'py'=4] {'px'}, dimensions={0} | all-to-all | bytes 16777216 | tf_op jit(solution)/shard_map/all_to_all | solution.py:147
  722.4 20.5 %fusion.125 = (f32[64,128,256]{2,1,0:T(8,128)S(1)}, f32[64,128,256]{2,1,0:T(8,128)}) fusion(f32[64,128,256]{2,1,0:T(8,128)} %param.41, f32[64,128,256]{1,2,0:T(8,128)S(1)} %bitcast.144, s32[256]{0:T(256)S(1)} %iota_add_fusion.1), kind=kOutput, calls=%fused_computation.198 | convolution fusion | flops 6445203456 | bytes 33555456 | tf_op jit(solution)/shard_map/abc,ck->abk/dot_general | solution.py:48
  745.6 34.8 %collective-permute-done.1 = f32[24,128,256]{2,1,0:T(8,128)S(1)} collective-permute-done((f32[24,128,256]{2,1,0:T(8,128)S(1)}, f32[24,128,256]{2,1,0:T(8,128)S(1)}, u32[]{:S(2)}, u32[]{:S(2)}) %collective-permute-start.1) | collective-permute-done | bytes 3145760 | tf_op jit(solution)/shard_map/ppermute | solution.py:20
  787.3 45.1 %collective-permute-done = s32[2]{0:T(128)S(1)} collective-permute-done((s32[2]{0:T(128)S(1)}, s32[2]{0:T(128)S(1)}, u32[]{:S(2)}, u32[]{:S(2)}) %collective-permute-start) | collective-permute-done | bytes 40 | tf_op jit(solution)/shard_map/ppermute | solution.py:24
  850.1 10.5 pad_maximum_fusion
  860.6 9.0 while.97
  874.9 24.2 %collective-permute-done.3 = f32[2,9,24,576]{3,2,0,1:T(8,128)S(1)} collective-permute-done((f32[2,9,24,576]{3,2,0,1:T(8,128)S(1)}, f32[2,9,24,576]{3,2,0,1:T(8,128)S(1)}, u32[]{:S(2)}, u32[]{:S(2)}) %collective-permute-start.3) | collective-permute-done | bytes 995360 | tf_op jit(solution)/shard_map/ppermute | solution.py:24
  902.4 31.4 %while.93 = (s32[]{:T(128)}, f32[2,8,24,576]{3,2,1,0:T(8,128)}, f32[2,8,24,576]{3,2,0,1:T(8,128)S(1)}, s32[2]{0:T(128)S(1)}, f32[2,24,576]{2,1,0:T(8,128)S(1)}, ...) while((s32[]{:T(128)}, f32[2,8,24,576]{3,2,1,0:T(8,128)}, ...), condition=%wide.region_7.8_spmd, body=%wide.region_1.7_spmd.sunk | while | flops 2575890 | bytes 12820806 | solution.py:102
  904.9 23.5 %while.98 = (s32[]{:T(128)}, f32[1,8,24,576]{3,2,1,0:T(8,128)S(1)}, f32[1,8,24,576]{3,2,1,0:T(8,128)S(1)}, s32[]{:T(128)}, s32[1]{0:T(128)}, /*index=5*/f32[1,1,...) while((s32[]{:T(128)}, f32[1,8,24,576]{3,2,1,0:T(8,128)S(1)}, ...), condition=%wide.region_5.5_spmd, body=%wide.region_4.4_spmd.sunk | while | flops 2216452 | bytes 9564041 | solution.py:90
  936.1 15.0 %collective-permute-start.4 = (f32[2,8,24,576]{3,2,1,0:T(8,128)}, f32[2,8,24,576]{3,2,1,0:T(8,128)}, u32[]{:S(2)}, u32[]{:S(2)}) collective-permute-start(f32[2,8,24,576]{3,2,1,0:T(8,128)} %broadcast_select_fusion.3), channel_id=1, source_target_pairs={{0,1},{1,0},{2,3},{3,2},{4,5},{5,4},{6,7},{7,6},{8,9},{9,8},{10,11... | collective-permute-start | bytes 2654216 | tf_op jit(solution)/shard_map/ppermute | solution.py:24
  951.2 65.6 %while.95 = (s32[]{:T(128)}, f32[2,8,24,576]{3,2,1,0:T(8,128)S(1)}, f32[2,8,24,576]{3,2,1,0:T(8,128)S(1)}, s32[2]{0:T(128)S(1)}, f32[2,24,576]{2,1,0:T(8,128)S(1...) while((s32[]{:T(128)}, f32[2,8,24,576]{3,2,1,0:T(8,128)S(1)}, ...), condition=%wide.region_14.15_spmd, body=%wide.region_8.14_spmd.sunk | while | flops 2575890 | bytes 12870438 | solution.py:102
  957.3 59.2 %while.99 = (s32[]{:T(128)}, f32[1,8,24,576]{3,2,1,0:T(8,128)S(1)}, f32[1,8,24,576]{3,2,1,0:T(8,128)S(1)}, s32[]{:T(128)}, s32[1]{0:T(128)}, /*index=5*/f32[1,1,...) while((s32[]{:T(128)}, f32[1,8,24,576]{3,2,1,0:T(8,128)S(1)}, ...), condition=%wide.region_12.12_spmd, body=%wide.region_11.11_spmd.sunk | while | flops 2216452 | bytes 9564041 | solution.py:90
  1019.2 5.9 broadcast_in_dim.189
  1025.1 42.0 %while.96 = (s32[]{:T(128)}, f32[88,152,256]{2,1,0:T(8,128)}, s32[2,3]{1,0:T(2,128)S(1)}, f32[2,24,576]{2,1,0:T(8,128)S(1)}, s32[]{:T(128)}, /*index=5*/s32[]{:T(128)}, s32[]{:T(128)}, s32[]{:T(128)}, s32[]{:T(128)}) while((s32[]{:T(128)}, f32[88,152,256]{2,1,0:T(8,128)}, s32[2,3]{1,0:T(2,128)S(1)}, f32[2,24,576]{2,1,0:T(8,128)S(1)}, ...), condition=%wide.region_17.18_spmd, body=%wide.region_16.17_spmd.sunk | while | flops 13835 | bytes 497915 | solution.py:213
  1032.9 12.6 %dynamic_update_slice.27 = f32[88,152,256]{2,1,0:T(8,128)} dynamic-update-slice(f32[88,152,256]{2,1,0:T(8,128)} %get-tuple-element.1236, f32[24,24,24]{2,1,0:T(8,128)S(1)} %dynamic-slice_add_fusion.2, s32[]{:T(128)S(6)} %select_n.434, s32[]{:T(128)S(6)} %select_n.435, s32[]{:T(128)S(6)} %select_n.436) | dynamic-update-slice | bytes 110596 | tf_op jit(solution)/shard_map/while/body/eval_jaxpr/dynamic_update_slice | solution.py:210
  1053.5 13.5 %dynamic_update_slice.27 = f32[88,152,256]{2,1,0:T(8,128)} dynamic-update-slice(f32[88,152,256]{2,1,0:T(8,128)} %get-tuple-element.1236, f32[24,24,24]{2,1,0:T(8,128)S(1)} %dynamic-slice_add_fusion.2, s32[]{:T(128)S(6)} %select_n.434, s32[]{:T(128)S(6)} %select_n.435, s32[]{:T(128)S(6)} %select_n.436) | dynamic-update-slice | bytes 110596 | tf_op jit(solution)/shard_map/while/body/eval_jaxpr/dynamic_update_slice | solution.py:210
  1072.0 10.9 broadcast_select_fusion.2
  1083.0 26.9 %collective-permute-done.5 = f32[88,24,256]{2,1,0:T(8,128)S(1)} collective-permute-done((f32[88,24,256]{2,1,0:T(8,128)}, f32[88,24,256]{2,1,0:T(8,128)S(1)}, u32[]{:S(2)}, u32[]{:S(2)}) %collective-permute-start.5) | collective-permute-done | bytes 2162720 | tf_op jit(solution)/shard_map/ppermute | solution.py:20
  1117.2 7.8 slice.344
  1129.7 24.2 %collective-permute-done.6 = f32[24,128,256]{2,1,0:T(8,128)} collective-permute-done((f32[24,128,256]{2,1,0:T(8,128)S(1)}, f32[24,128,256]{2,1,0:T(8,128)}, u32[]{:S(2)}, u32[]{:S(2)}) %collective-permute-start.6) | collective-permute-done | bytes 3145760 | tf_op jit(solution)/shard_map/ppermute | solution.py:20
  (287 shorter events, 145.2 us)
Async XLA Ops:
  28.8 98.1 %all-to-all-start = ((f32[64,128,256]{1,0,2:T(8,128)}), f32[64,128,256]{1,0,2:T(8,128)}, u32[]{:S(2)}, u32[]{:S(2)}) async-start(f32[64,128,256]{1,0,2:T(8,128)} %copy.36), calls=%async_computation | async-start | bytes 16777216 | tf_op jit(solution)/shard_map/all_to_all | solution.py:131
  158.1 186.2 %all-to-all-start.1 = ((f32[512,128,32]{1,2,0:T(8,128)}), f32[512,128,32]{1,2,0:T(8,128)}, u32[]{:S(2)}, u32[]{:S(2)}) async-start(f32[512,128,32]{1,2,0:T(8,128)} %copy.38), calls=%async_computation.1 | async-start | bytes 16777216 | tf_op jit(solution)/shard_map/all_to_all | solution.py:134
  742.9 38.9 %copy-start = (f32[64,128,256]{2,1,0:T(8,128)}, f32[64,128,256]{2,1,0:T(8,128)S(1)}, u32[]{:S(2)}) copy-start(f32[64,128,256]{2,1,0:T(8,128)S(1)} %get-tuple-element.759) | copy-start | bytes 25165828
  743.2 41.5 %copy-start.8 = (s32[2]{0:T(128)S(1)}, s32[2]{0:T(128)}, u32[]{:S(2)}) copy-start(s32[2]{0:T(128)} %param.45) | copy-start | bytes 28
  743.2 43.9 %copy-start.5 = (s32[2,3]{1,0:T(2,128)S(1)}, s32[2,3]{1,0:T(2,128)}, u32[]{:S(2)}) copy-start(s32[2,3]{1,0:T(2,128)} %param.43) | copy-start | bytes 76
  743.3 100.4 %copy-start.4 = (s32[2]{0:T(128)S(1)}, s32[2]{0:T(128)}, u32[]{:S(2)}) copy-start(s32[2]{0:T(128)} %constant.648.clone.1) | copy-start | bytes 28
  743.3 37.0 %collective-permute-start.1 = (f32[24,128,256]{2,1,0:T(8,128)S(1)}, f32[24,128,256]{2,1,0:T(8,128)S(1)}, u32[]{:S(2)}, u32[]{:S(2)}) collective-permute-start(f32[24,128,256]{2,1,0:T(8,128)S(1)} %slice.340), channel_id=1, source_target_pairs={{4,0},{8,4},{12,8},{16,12},{20,16},{24,20},{28,24},{5,1},{9,5},{13... | collective-permute-start | bytes 9437192 | tf_op jit(solution)/shard_map/ppermute | solution.py:20
  781.9 68.3 %collective-permute-start.2 = (f32[88,24,256]{2,1,0:T(8,128)}, f32[88,24,256]{2,1,0:T(8,128)}, u32[]{:S(2)}, u32[]{:S(2)}) collective-permute-start(f32[88,24,256]{2,1,0:T(8,128)} %pad_maximum_fusion.1), channel_id=1, source_target_pairs={{1,0},{2,1},{3,2},{5,4},{6,5},{7,6},{9,8},{10,9},{11,10},{13,12},{... | collective-permute-start | bytes 6488072 | tf_op jit(solution)/shard_map/ppermute | solution.py:20
  784.7 47.6 %collective-permute-start = (s32[2]{0:T(128)S(1)}, s32[2]{0:T(128)S(1)}, u32[]{:S(2)}, u32[]{:S(2)}) collective-permute-start(s32[2]{0:T(128)S(1)} %copy-done.8), channel_id=1, source_target_pairs={{0,1},{1,0},{2,3},{3,2},{4,5},{5,4},{6,7},{7,6},{8,9},{9,8},{10,11... | collective-permute-start | bytes 32 | tf_op jit(solution)/shard_map/ppermute | solution.py:24
  850.1 20.8 %copy-start.6 = (pred[2]{0:T(512)(128)(4,1)}, pred[2]{0:T(512)(128)(4,1)S(1)}, u32[]{:S(2)}) copy-start(pred[2]{0:T(512)(128)(4,1)S(1)} %get-tuple-element.754) | copy-start | bytes 10
  850.1 22.9 %copy-start.11 = (s32[2]{0:T(128)S(1)}, s32[2]{0:T(128)}, u32[]{:S(2)}) copy-start(s32[2]{0:T(128)} %param.44) | copy-start | bytes 28
  872.3 26.8 %collective-permute-start.3 = (f32[2,9,24,576]{3,2,0,1:T(8,128)S(1)}, f32[2,9,24,576]{3,2,0,1:T(8,128)S(1)}, u32[]{:S(2)}, u32[]{:S(2)}) collective-permute-start(f32[2,9,24,576]{3,2,0,1:T(8,128)S(1)} %maximum_select_fusion), channel_id=1, source_target_pairs={{0,1},{1,0},{2,3},{3,2},{4,5},{5,4},{6,7},{7,6},{8,9},{9,8},{10,11... | collective-permute-start | bytes 2985992 | tf_op jit(solution)/shard_map/ppermute | solution.py:24
  899.1 1.0 copy-start.2
  902.4 48.8 %copy-start.1 = (f32[2,8,24,576]{3,2,1,0:T(8,128)S(1)}, f32[2,8,24,576]{3,2,1,0:T(8,128)}, u32[]{:S(2)}) copy-start(f32[2,8,24,576]{3,2,1,0:T(8,128)} %param.42) | copy-start | bytes 2654212
  936.1 80.6 %collective-permute-start.4 = (f32[2,8,24,576]{3,2,1,0:T(8,128)}, f32[2,8,24,576]{3,2,1,0:T(8,128)}, u32[]{:S(2)}, u32[]{:S(2)}) collective-permute-start(f32[2,8,24,576]{3,2,1,0:T(8,128)} %broadcast_select_fusion.3), channel_id=1, source_target_pairs={{0,1},{1,0},{2,3},{3,2},{4,5},{5,4},{6,7},{7,6},{8,9},{9,8},{10,11... | collective-permute-start | bytes 2654216 | tf_op jit(solution)/shard_map/ppermute | solution.py:24
  951.1 65.6 %copy-start.7 = (pred[2]{0:T(512)(128)(4,1)S(1)}, pred[2]{0:T(512)(128)(4,1)}, u32[]{:S(2)}) copy-start(pred[2]{0:T(512)(128)(4,1)} %copy-done.6) | copy-start | bytes 10
  951.1 68.0 %copy-start.10 = (f32[2]{0:T(128)S(1)}, f32[2]{0:T(128)}, u32[]{:S(2)}) copy-start(f32[2]{0:T(128)} %convert_multiply_fusion) | copy-start | bytes 28
  1016.7 8.3 copy-start.3
  1025.1 47.0 %copy-start.9 = (pred[152]{0:T(512)(128)(4,1)S(1)}, pred[152]{0:T(512)(128)(4,1)}, u32[]{:S(2)}) copy-start(pred[152]{0:T(512)(128)(4,1)} %constant.655.clone.1) | copy-start | bytes 460
  1070.1 39.7 %collective-permute-start.5 = (f32[88,24,256]{2,1,0:T(8,128)}, f32[88,24,256]{2,1,0:T(8,128)S(1)}, u32[]{:S(2)}, u32[]{:S(2)}) collective-permute-start(f32[88,24,256]{2,1,0:T(8,128)} %slice.320), channel_id=1, source_target_pairs={{0,1},{1,2},{2,3},{4,5},{5,6},{6,7},{8,9},{9,10},{10,11},{12,13},{... | collective-permute-start | bytes 6488072 | tf_op jit(solution)/shard_map/ppermute | solution.py:20
  1115.2 38.7 %collective-permute-start.6 = (f32[24,128,256]{2,1,0:T(8,128)S(1)}, f32[24,128,256]{2,1,0:T(8,128)}, u32[]{:S(2)}, u32[]{:S(2)}) collective-permute-start(f32[24,128,256]{2,1,0:T(8,128)S(1)} %slice.346), channel_id=1, source_target_pairs={{0,4},{4,8},{8,12},{12,16},{16,20},{20,24},{24,28},{1,5},{5,9},{9,... | collective-permute-start | bytes 9437192 | tf_op jit(solution)/shard_map/ppermute | solution.py:20
where the time goes:
time: 1170 us; the launch traced here: 1160 us
  waiting for transfers between devices  428 us (37%)
  blocking collectives  284 us (24%)
  local copies, waits for them, and re-layouts  141 us (12%)
  matrix products  122 us (10%)
  other arithmetic  77.8 us (7%)
  loops' own time  60.9 us (5%)
  starting transfers between devices  37.6 us (3%)
    all_to_all x1, blocking collectives, solve_rows(): lax.all_to_all(spectrum, 'py', split_axis=1, concat_axis=0, tiled=True)  188 us
    all_to_all x1, waiting for transfers between devices, solve_rows(): lax.all_to_all(spectrum, 'py', split_axis=0, concat_axis=1, tiled=True)  180 us
    all_to_all x1, blocking collectives, solve_rows(): lax.all_to_all(spectrum, 'px', split_axis=0, concat_axis=2, tiled=True)  95.8 us
    all_to_all x1, waiting for transfers between devices, solve_rows(): lax.all_to_all(spectrum, 'px', split_axis=2, concat_axis=0, tiled=True)  92.5 us
    ppermute x4, waiting for transfers between devices, shifted(): return lax.ppermute(x, axis, pairs)  85.9 us
    ppermute x3, waiting for transfers between devices, partner(): lax.ppermute(x, axis, [(i, i ^ 1 << bit) for i in range(lax.axis_size(axi...  69.3 us
    another operation x4, loops' own time, chebyshev(): lax.fori_loop(0, steps, advance, (orbital_set, orbital_set))  44.2 us
    dot_general x2, matrix products, along_second(): return jnp.einsum('abc,bk->akc', field, table, precision=highest)  41.1 us
  transfers between devices with their start and end apart: 9, of which 7 were waited for; matrix products, arithmetic and copies ran while one was open for 6% of the time, Pallas kernels for 0%

commit v1 on v0

v1 whole, which is shorter than its diff:
```python
import functools

import jax
import jax.numpy as jnp
import ml_dtypes
import numpy as np
from jax import lax
from jax.experimental import pallas as pl
from jax.experimental.pallas import tpu as pltpu
from jax.sharding import PartitionSpec as P

screening = 0.002
window_gap = 0.1
kinetic_top = 6.0
highest = lax.Precision.HIGHEST
vmem_bytes = 56 * 1024 * 1024
f32 = jnp.float32
bf16 = jnp.bfloat16


def sine_table(length):
    index = np.arange(1, length + 1, dtype=np.int64)
    product = index[:, None] * index[None, :] % (2 * length + 2)
    return np.sin(np.pi * product / (length + 1)) * np.sqrt(2.0 / (length + 1))


def eigen_values(length):
    index = np.arange(1, length + 1, dtype=np.float64)
    return 4.0 * np.sin(np.pi * index / (2 * (length + 1))) ** 2


def decay(shift):
    return 2.0 * np.arcsinh(0.5 * np.sqrt(shift))


def halves(table):
    high = table.astype(np.float32).astype(ml_dtypes.bfloat16)
    low = (table - high.astype(np.float64)).astype(np.float32).astype(ml_dtypes.bfloat16)
    return high, low


def split(value):
    high = value.astype(bf16)
    return high, (value - high.astype(f32)).astype(bf16)


def dot(left, right):
    return jnp.dot(left, right, preferred_element_type=f32)


def third_product(value, high_ref, low_ref):
    high, low = split(value)
    return dot(high, high_ref[...]) + (dot(high, low_ref[...]) + dot(low, high_ref[...]))


def second_product(value, table_ref):
    rows = value.shape[0]
    both = dot(table_ref[...], jnp.concatenate(split(value), 0))
    return both[:rows] + both[rows:]


def rows_of(count):
    return min(32, count)


def forward_kernel(
    x_ref, zh_ref, zl_ref, sy_ref, r_ref, s0_ref, s1_ref, p_ref, w_ref, carry, left, right
):
    step = pl.program_id(0)
    slabs, cols, depth = x_ref.shape
    rows = p_ref.shape[0]

    @pl.when(step == 0)
    def _():
        carry[...] = jnp.zeros_like(carry)

    turned = third_product(x_ref[...].reshape(slabs * cols, depth), zh_ref, zl_ref)
    for slab in range(slabs):
        value = second_product(turned[slab * cols : (slab + 1) * cols], sy_ref)
        value = r_ref[...] * carry[...] + value
        carry[...] = value
        p_ref[step * slabs + slab] = value

    @pl.when(step == pl.num_programs(0) - 1)
    def _():
        left[...] = jnp.zeros_like(left)
        right[...] = jnp.zeros_like(right)
        part = rows_of(cols)
        for start in range(0, cols, part):
            span = pl.ds(start, part)
            ratio = r_ref[span, :]
            first = s0_ref[span, :]
            last = s1_ref[span, :]

            def back(count, u):
                row = rows - 1 - count
                u = ratio * (u + p_ref[row, span, :])
                left[row] += jnp.sum((first * u).reshape(part // 8, 8, depth), 0)
                right[row] += jnp.sum((last * u).reshape(part // 8, 8, depth), 0)
                return u

            u = lax.fori_loop(0, rows, back, jnp.zeros((part, depth), f32))
            w_ref[pl.ds(2 * rows + cols + start, part), :] = u
        w_ref[pl.ds(0, rows), :] = jnp.sum(left[...], 1)
        w_ref[pl.ds(rows, rows), :] = jnp.sum(right[...], 1)
        w_ref[pl.ds(2 * rows, cols), :] = carry[...]


def backward_kernel(
    p_ref, w_ref, zh_ref, zl_ref, sy_ref, r_ref, s0_ref, s1_ref, out_ref, q, carry, turned
):
    step = pl.program_id(0)
    steps = pl.num_programs(0)
    slabs, cols, depth = out_ref.shape
    rows = p_ref.shape[0]

    @pl.when(step == 0)
    def _():
        part = rows_of(cols)
        for start in range(0, cols, part):
            span = pl.ds(start, part)
            ratio = r_ref[span, :]
            first = s0_ref[span, :]
            last = s1_ref[span, :]

            def ahead(row, p):
                lower = w_ref[pl.ds(row, 1), :]
                upper = w_ref[pl.ds(rows + row, 1), :]
                p = ratio * p + (first * lower + last * upper)
                q[row, span, :] = p_ref[row, span, :] + p
                return p

            lax.fori_loop(0, rows, ahead, w_ref[pl.ds(2 * rows + start, part), :])
        carry[...] = w_ref[pl.ds(2 * rows + cols, cols), :]

    base = (steps - 1 - step) * slabs
    for slab in range(slabs - 1, -1, -1):
        u = r_ref[...] * (carry[...] + q[base + slab])
        carry[...] = u
        turned[slab] = second_product(u, sy_ref)
    value = third_product(turned[...].reshape(slabs * cols, depth), zh_ref, zl_ref)
    out_ref[...] = value.reshape(slabs, cols, depth)


def whole(shape):
    return pl.BlockSpec(shape, lambda step: (0,) * len(shape))


def params():
    return pltpu.CompilerParams(vmem_limit_bytes=vmem_bytes)


def hartree(density, peers_x, peers_y):
    rows, cols, depth = density.shape
    span_x = rows * peers_x
    devices = peers_x * peers_y
    chunk = -(-depth // devices)
    padded = chunk * devices
    slabs = min(8, rows)
    steps = rows // slabs
    z_high, z_low = halves(sine_table(depth))
    y_table = sine_table(cols)
    y_high, y_low = halves(y_table)
    y_both = np.block([[y_high, y_high], [y_low, y_low]])
    z_values = np.pad(eigen_values(depth), (0, padded - depth), mode="edge")
    block_shift = eigen_values(cols)[None, :] + z_values[:, None] + screening
    theta_all = decay(block_shift)
    ratio = np.exp(-theta_all[:depth].T).astype(np.float32)
    first = y_table[0].astype(np.float32)
    last = y_table[-1].astype(np.float32)
    first_wide = np.broadcast_to(first[:, None], (cols, depth)).copy()
    last_wide = np.broadcast_to(last[:, None], (cols, depth)).copy()
    edge_theta = decay(eigen_values(span_x)[None, :] + z_values[:, None] + screening)
    edge_near = np.exp(-edge_theta) * np.expm1(-2 * cols * edge_theta)
    edge_near = (edge_near / np.expm1(-2 * (cols + 1) * edge_theta)).astype(np.float32)
    edge_far = np.exp(-cols * edge_theta) * np.expm1(-2 * edge_theta)
    edge_far = (edge_far / np.expm1(-2 * (cols + 1) * edge_theta)).astype(np.float32)
    width = 2 * rows + 2 * cols
    tables = (z_high, z_low, y_both, ratio, first_wide, last_wide)
    table_specs = [whole(table.shape) for table in tables]

    p, edges = pl.pallas_call(
        forward_kernel,
        grid=(steps,),
        in_specs=[pl.BlockSpec((slabs, cols, depth), lambda step: (step, 0, 0))] + table_specs,
        out_specs=[whole((rows, cols, depth)), whole((width, depth))],
        out_shape=[
            jax.ShapeDtypeStruct((rows, cols, depth), f32),
            jax.ShapeDtypeStruct((width, depth), f32),
        ],
        scratch_shapes=[
            pltpu.VMEM((cols, depth), f32),
            pltpu.VMEM((rows, 8, depth), f32),
            pltpu.VMEM((rows, 8, depth), f32),
        ],
        compiler_params=params(),
        name="solve_ahead",
    )(density, *tables)

    owner = lax.axis_index("px") * peers_y + lax.axis_index("py")

    def owned(table):
        return lax.dynamic_slice_in_dim(jnp.asarray(table), owner * chunk, chunk, 0)

    theta = owned(theta_all.astype(np.float32))
    r = jnp.exp(-theta)
    gap = -jnp.expm1(-2.0 * theta)
    block_power = jnp.exp(-rows * theta)
    spread = r * r * -jnp.expm1(-2.0 * rows * theta) / gap
    closing = gap / -jnp.expm1(-2.0 * (span_x + 1) * theta)
    place = jnp.arange(rows, dtype=f32)[None, :, None]
    to_end = jnp.exp(-theta[:, None, :] * (rows - 1 - place))
    to_start = (
        jnp.exp(-theta[:, None, :] * (place + 1))
        * -jnp.expm1(-2.0 * theta[:, None, :] * (rows - place))
        / gap[:, None, :]
    )
    near = owned(edge_near)
    far = owned(edge_far)
    table_x = jnp.asarray(sine_table(span_x).astype(np.float32))

    def carries(ends, starts):
        entering = [jnp.zeros_like(ends[0])]
        for i in range(1, peers_x):
            entering.append(ends[i - 1] + block_power * entering[-1])

        def sweep(entering):
            values = [jnp.zeros_like(ends[0])]
            for i in range(peers_x - 1, -1, -1):
                values.append(starts[i] + spread * entering[i] + block_power * values[-1])
            return values[::-1]

        mirror = -closing * sweep(entering)[0]
        fixed = []
        for i in range(peers_x):
            fixed.append(entering[i] + mirror)
            mirror = block_power * mirror
        return jnp.stack(fixed), jnp.stack(sweep(fixed)[1:])

    sent = jnp.pad(edges.T, ((0, padded - depth), (0, 0))).reshape(devices, chunk, width)
    held = lax.all_to_all(sent, ("px", "py"), split_axis=0, concat_axis=0, tiled=True)
    held = held.reshape(peers_x, peers_y, chunk, width)
    ends = held[..., 2 * rows : 2 * rows + cols]
    starts = held[..., 2 * rows + cols :]
    entering, leaving = carries(ends, starts)
    sides = jnp.stack([jnp.asarray(first), jnp.asarray(last)])[:, None, None, None, :]
    edge_values = jnp.stack([held[..., :rows], held[..., rows : 2 * rows]])
    edge_values = (
        edge_values
        + jnp.einsum("sijck,cxk->sijcx", sides * (r * entering), to_start, precision=highest)
        + jnp.einsum("sijck,cxk->sijcx", sides * (r * leaving), to_end, precision=highest)
    )
    lines = edge_values.transpose(0, 2, 3, 1, 4).reshape(2, peers_y, chunk, span_x)
    lines = jnp.einsum("sjcx,xk->sjck", lines, table_x, precision=highest)
    known = jnp.zeros_like(near)
    slope = jnp.zeros_like(near)
    steps_back = []
    for j in range(peers_y):
        scale = 1.0 / (1.0 - near * slope)
        middle = (lines[0, j] + near * known) * scale
        steps_back.append((middle, far * scale, known, slope))
        known = lines[1, j] + far * (known + slope * middle)
        slope = near + far * slope * far * scale
    above = jnp.zeros_like(near)
    lower = []
    upper = []
    for j in range(peers_y - 1, -1, -1):
        middle, reach, known, slope = steps_back[j]
        upper.append(above)
        above = middle + reach * above
        lower.append(known + slope * above)
    outer = jnp.stack([jnp.stack(lower[::-1]), jnp.stack(upper[::-1])])
    outer = jnp.einsum("sjck,xk->sjcx", outer, table_x, precision=highest)
    outer = outer.reshape(2, peers_y, chunk, peers_x, rows).transpose(0, 3, 1, 2, 4)
    more_ends = jnp.sum(
        sides * jnp.einsum("sijcx,cxk->sijck", outer, to_end, precision=highest), 0
    )
    more_starts = jnp.sum(
        sides * jnp.einsum("sijcx,cxk->sijck", outer, to_start, precision=highest), 0
    )
    entering, leaving = carries(ends + more_ends, starts + more_starts)
    answer = jnp.concatenate([outer[0], outer[1], entering, leaving], -1)
    answer = answer.reshape(devices, chunk, width)
    answer = lax.all_to_all(answer, ("px", "py"), split_axis=0, concat_axis=0, tiled=True)
    answer = answer.reshape(padded, width)[:depth].T

    return pl.pallas_call(
        backward_kernel,
        grid=(steps,),
        in_specs=[whole((rows, cols, depth)), whole((width, depth))] + table_specs,
        out_specs=pl.BlockSpec((slabs, cols, depth), lambda step: (steps - 1 - step, 0, 0)),
        out_shape=jax.ShapeDtypeStruct((rows, cols, depth), f32),
        scratch_shapes=[
            pltpu.VMEM((rows, cols, depth), f32),
            pltpu.VMEM((cols, depth), f32),
            pltpu.VMEM((slabs, cols, depth), f32),
        ],
        compiler_params=params(),
        name="solve_back",
    )(p, answer, *tables)


def cut_kernel(edge, corner_ref, field_ref, other_ref, out_ref, held, sems):
    rows, cols, depth = field_ref.shape
    count, _, wide, tall, _ = held.shape

    def corner(index):
        return corner_ref[index, 0], corner_ref[index, 1], corner_ref[index, 2]

    def meets(index):
        x, y, _ = corner(index)
        return (x > -edge) & (x < rows) & (y > -edge) & (y < cols)

    def window(index):
        x, y, _ = corner(index)
        x_start = jnp.clip(x, 0, rows - wide)
        y_start = jnp.clip(jnp.maximum(y, 0) // 8 * 8, 0, cols - tall)
        return x_start, pl.multiple_of(y_start, 8)

    def copies(index):
        x_start, y_start = window(index)
        return [
            pltpu.make_async_copy(
                source.at[pl.ds(x_start, wide), pl.ds(y_start, tall), :],
                held.at[index, which],
                sems.at[index, which],
            )
            for which, source in enumerate((field_ref, other_ref))
        ]

    for index in range(count):

        @pl.when(meets(index))
        def _():
            for copy in copies(index):
                copy.start()

    for index in range(count):

        @pl.when(jnp.logical_not(meets(index)))
        def _():
            out_ref[index] = jnp.zeros(out_ref.shape[1:], f32)

        @pl.when(meets(index))
        def _():
            for copy in copies(index):
                copy.wait()
            x, y, z = corner(index)
            x_start, y_start = window(index)
            turn_y = lax.rem(y_start - y + tall, tall)
            turn_z = lax.rem(depth - z, depth)
            place = y + lax.broadcasted_iota(jnp.int32, (edge, edge), 0)
            inside = (place >= 0) & (place < cols)

            def one(k, _):
                row = jnp.clip(x + k, 0, rows - 1) - x_start
                value = held[index, 0, row] + held[index, 1, row]
                value = pltpu.roll(value, turn_y, 0)
                value = pltpu.roll(value, turn_z, 1)
                here = (x + k >= 0) & (x + k < rows)
                out_ref[index, k] = jnp.where(inside & here, value[:edge, :edge], 0.0)
                return 0

            lax.fori_loop(0, edge, one, 0)


def filter_kernel(
    degree_ref, weight_ref, box_ref, orbital_ref, out_ref, share_ref, state, slope_ref
):
    which = pl.program_id(0)
    _, orbitals, edge, merged = orbital_ref.shape
    lanes = state.shape[-1]
    box = box_ref[0]
    low = jnp.min(box) + window_gap
    high = jnp.max(box) + kinetic_top
    centre = 0.5 * (high + low)
    lane = lax.broadcasted_iota(jnp.int32, (orbitals, lanes), 1)
    inner = lax.rem(lane, edge)
    not_low = inner != 0
    not_high = inner != edge - 1
    inverse = 2.0 / (high - low + jnp.zeros((orbitals, lanes), f32))
    hop = jnp.where(lane < merged, -inverse, 0.0)
    state[...] = jnp.zeros_like(state)
    slope_ref[...] = jnp.zeros_like(slope_ref)
    state[0, 1 : edge + 1, :, :merged] = jnp.swapaxes(orbital_ref[0], 0, 1)
    for x in range(edge):
        row = (3.0 - centre + box[x : x + 1]) * (2.0 * inverse[:1, :merged])
        slope_ref[x, :, :merged] = jnp.broadcast_to(row, (orbitals, merged))

    def image(source, x, before, current, after):
        total = before + after
        total = total + pltpu.roll(current, edge, 1) + pltpu.roll(current, lanes - edge, 1)
        total = total + pltpu.roll(jnp.where(not_high, current, 0.0), 1, 1)
        total = total + pltpu.roll(jnp.where(not_low, current, 0.0), lanes - 1, 1)
        return slope_ref[x] * current + hop * total

    def advance(source, target, opening):
        before = state[source, 0]
        current = state[source, 1]
        for x in range(edge):
            after = state[source, x + 2]
            value = image(source, x, before, current, after)
            if opening:
                state[target, x + 1] = 0.5 * value
            else:
                state[target, x + 1] = value - state[target, x + 1]
            before, current = current, after

    degree = degree_ref[which]

    @pl.when(degree > 0)
    def _():
        advance(0, 1, True)

    def both(count, _):
        advance(1, 0, False)
        advance(0, 1, False)
        return 0

    lax.fori_loop(0, lax.div(degree - 1, 2), both, 0)
    even = lax.rem(degree, 2) == 0

    @pl.when(even & (degree > 0))
    def _():
        advance(1, 0, False)

    final = jnp.where(even, 0, 1)
    squares = jnp.zeros((orbitals, lanes), f32)
    for x in range(edge):
        value = state[final, x + 1]
        squares = squares + value * value
    total = jnp.sum(squares, axis=1, keepdims=True)
    scale = jnp.sqrt(edge**3 / (total + 1e-06))
    weight = weight_ref[which].astype(f32) / orbitals
    for x in range(edge):
        value = state[final, x + 1] * scale
        state[final, x + 1] = value
        share = weight * jnp.sum(value * value, axis=0, keepdims=True)
        share_ref[0, x : x + 1] = share[:, :merged]
    out_ref[0] = jnp.swapaxes(state[final, 1 : edge + 1], 0, 1)[:, :, :merged]


def patch_kernel(edge, margin, corner_ref, share_ref, out_ref, total, sem):
    rows, cols, depth = out_ref.shape
    count, _, tall, lanes = share_ref.shape

    def clear(row, _):
        total[row] = jnp.zeros(total.shape[1:], f32)
        return 0

    lax.fori_loop(0, rows, clear, 0)
    for index in range(count):
        x = corner_ref[index, 0]
        y = corner_ref[index, 1]
        z = corner_ref[index, 2]

        @pl.when((x > -edge) & (x < rows) & (y > -edge) & (y < cols))
        def _():
            start = (y + margin) // 8 * 8
            turn = y + margin - start
            span = pl.ds(pl.multiple_of(start, 8), tall)

            def one(k, _):
                value = share_ref[index, k]
                if depth > lanes:
                    value = jnp.concatenate([value, jnp.zeros((tall, depth - lanes), f32)], 1)
                value = pltpu.roll(value, turn, 0)
                value = pltpu.roll(value, z, 1)
                total[x + k, span, :] += value
                return 0

            lax.fori_loop(jnp.maximum(0, -x), jnp.minimum(edge, rows - x), one, 0)

    copy = pltpu.make_async_copy(total.at[:, pl.ds(margin, cols), :], out_ref, sem)
    copy.start()
    copy.wait()


def body(density, external, orbitals, anchors, weights, degrees):
    rows, cols, depth = density.shape
    count, orbital_count, edge, merged = orbitals.shape
    peers_x = lax.axis_size("px")
    peers_y = lax.axis_size("py")
    hops = [
        (a, b)
        for a in range((rows + edge - 2) // rows + 1)
        for b in range((cols + edge - 2) // cols + 1)
    ]

    def moved(value, a, b):
        if a == 0 and b == 0:
            return value
        pairs = [
            (i * peers_y + j, (i + a) * peers_y + j + b)
            for i in range(peers_x)
            for j in range(peers_y)
            if 0 <= i + a < peers_x and 0 <= j + b < peers_y
        ]
        return lax.ppermute(value, ("px", "py"), pairs)

    corners = jnp.concatenate([moved(anchors, a, b) for a, b in hops], 0)
    origin = jnp.stack([lax.axis_index("px") * rows, lax.axis_index("py") * cols, 0])
    corners = corners - origin[None, :].astype(jnp.int32)
    total = count * len(hops)

    field = hartree(density, peers_x, peers_y)

    scalars = pl.BlockSpec(memory_space=pltpu.SMEM)
    vectors = pl.BlockSpec(memory_space=pltpu.VMEM)
    anywhere = pl.BlockSpec(memory_space=pl.ANY)
    tall = -(-(edge + 7) // 8) * 8
    wide = min(edge, rows)
    pieces = pl.pallas_call(
        functools.partial(cut_kernel, edge),
        in_specs=[scalars, anywhere, anywhere],
        out_specs=vectors,
        out_shape=jax.ShapeDtypeStruct((total, edge, edge, edge), f32),
        scratch_shapes=[
            pltpu.VMEM((total, 2, wide, tall, depth), f32),
            pltpu.SemaphoreType.DMA((total, 2)),
        ],
        compiler_params=params(),
        name="cut_boxes",
    )(corners, field, external)
    pieces = pieces.reshape(len(hops), count, edge, merged)
    boxes = sum(moved(pieces[index], -a, -b) for index, (a, b) in enumerate(hops))

    lanes = -(-(merged + edge) // 128) * 128
    filtered, shares = pl.pallas_call(
        filter_kernel,
        grid=(count,),
        in_specs=[
            scalars,
            scalars,
            pl.BlockSpec((1, edge, merged), lambda f: (f, 0, 0)),
            pl.BlockSpec((1, orbital_count, edge, merged), lambda f: (f, 0, 0, 0)),
        ],
        out_specs=[
            pl.BlockSpec((1, orbital_count, edge, merged), lambda f: (f, 0, 0, 0)),
            pl.BlockSpec((1, edge, merged), lambda f: (f, 0, 0)),
        ],
        out_shape=[
            jax.ShapeDtypeStruct(orbitals.shape, f32),
            jax.ShapeDtypeStruct((count, edge, merged), f32),
        ],
        scratch_shapes=[
            pltpu.VMEM((2, edge + 2, orbital_count, lanes), f32),
            pltpu.VMEM((edge, orbital_count, lanes), f32),
        ],
        compiler_params=params(),
        name="filter_orbitals",
    )(degrees, weights, boxes, orbitals)

    parts = jnp.concatenate([moved(shares, a, b) for a, b in hops], 0)
    parts = parts.reshape(total, edge, edge, edge)
    side = min(128, depth)
    parts = jnp.pad(parts, ((0, 0), (0, 0), (0, tall - edge), (0, side - edge)))
    margin = tall
    new_density = pl.pallas_call(
        functools.partial(patch_kernel, edge, margin),
        in_specs=[scalars, vectors],
        out_specs=anywhere,
        out_shape=jax.ShapeDtypeStruct(density.shape, f32),
        scratch_shapes=[
            pltpu.VMEM((rows, cols + 2 * margin, depth), f32),
            pltpu.SemaphoreType.DMA,
        ],
        compiler_params=params(),
        name="patch_density",
    )(corners, parts)
    return (field, filtered, new_density)


def solution(mesh):
    placed = (
        P("px", "py", None),
        P("px", "py", None),
        P(("px", "py"), None, None, None),
        P(("px", "py"), None),
        P(("px", "py")),
        P(("px", "py")),
    )
    return jax.shard_map(
        body,
        mesh=mesh,
        in_specs=placed,
        out_specs=(P("px", "py", None), P(("px", "py"), None, None, None), P("px", "py", None)),
        check_vma=False,
    )
```

time: 1170 us -> 174 us (0.15)
  the two profiles are of different devices: /device:TPU:18 before, /device:TPU:0 now
where the time goes in v1:
time: 174 us; the launch traced here: 175 us
  Pallas kernels  97.7 us (56%)
  starting transfers between devices  34 us (20%)
  waiting for transfers between devices  21.8 us (13%)
  local copies, waits for them, and re-layouts  9.21 us (5%)
  other arithmetic  6.09 us (4%)
  matrix products  4.41 us (3%)
    ppermute x9, starting transfers between devices, moved(): return lax.ppermute(value, ('px', 'py'), pairs)  22.8 us
    pallas_call x1, Pallas kernels, body(): pl.pallas_call(filter_kernel, grid=(count,), in_specs=[scalars, scalars,...  22.6 us
    pallas_call x1, Pallas kernels, body(): pl.pallas_call(functools.partial(patch_kernel, edge, margin), in_specs=[s...  20.5 us
    pallas_call x1, Pallas kernels, body(): pl.pallas_call(functools.partial(cut_kernel, edge), in_specs=[scalars, an...  19.9 us
    pallas_call x1, Pallas kernels, hartree(): pl.pallas_call(forward_kernel, grid=(steps,), in_specs=[pl.BlockSpec((sla...  19 us
    pallas_call x1, Pallas kernels, hartree(): pl.pallas_call(backward_kernel, grid=(steps,), in_specs=[whole((rows, col...  15.6 us
    all_to_all x1, waiting for transfers between devices, hartree(): lax.all_to_all(sent, ('px', 'py'), split_axis=0, concat_axis=0, tiled=True)  11 us
    ppermute x9, waiting for transfers between devices, moved(): return lax.ppermute(value, ('px', 'py'), pairs)  10.7 us
  transfers between devices with their start and end apart: 11, of which 5 were waited for; matrix products, arithmetic and copies ran while one was open for 1% of the time, Pallas kernels for 0%

profile of v1, /device:TPU:0, one launch (start us, length us, event | category | flops | bytes accessed | tf_op | source)
XLA Modules:
  0.0 174.5 jit_solution(7339034669009065606)
XLA Ops:
  0.7 19.0 %solve_ahead.1 = (f32[64,128,256]{2,1,0:T(8,128)}, f32[384,256]{1,0:T(8,128)}) custom-call(f32[64,128,256]{2,1,0:T(8,128)} %x_ref.1, bf16[256,256]{1,0:T(8,128)(2,1)} %constant.28.clone.zh_ref, bf16[256,256]{1,0:T(8,128)(2,1)} %constant.29.clone.zl_ref, bf16[256,256]{1,0:T(8,128)(2,1)} %constant.72.clone.sy_ref, f32[128,256]{1,0:T(8,128)} %constant.73.clone.r_ref, ...), custom_call_target="tpu_custom_call" | custom-call | tf_op jit(solution)/shard_map/solve_ahead/pallas_call | solution.py:182
  19.7 1.9 %copy.61 = f32[256,384]{1,0:T(8,128)} copy(f32[256,384]{0,1:T(8,128)} %bitcast.182) | data formatting | bytes 786432 | tf_op jit(solution)/shard_map/transpose | solution.py:240
  21.6 7.3 %all-to-all-start = ((f32[32,8,384]{2,1,0:T(8,128)}), f32[32,8,384]{2,1,0:T(8,128)S(1)}, u32[]{:S(2)}, u32[]{:S(2)}) async-start(f32[32,8,384]{2,1,0:T(8,128)} %bitcast.1), calls=%async_computation | async-start | bytes 786432 | tf_op jit(solution)/shard_map/all_to_all | solution.py:241
  29.7 11.0 %all-to-all-done = f32[32,8,384]{2,1,0:T(8,128)S(1)} async-done(((f32[32,8,384]{2,1,0:T(8,128)}), f32[32,8,384]{2,1,0:T(8,128)S(1)}, u32[]{:S(2)}, u32[]{:S(2)}) %all-to-all-start) | async-done | bytes 393248 | tf_op jit(solution)/shard_map/all_to_all | solution.py:241
  43.0 0.8 fusion.33
  43.9 0.8 fusion.56
  44.6 0.8 add_bitcast_fusion.2
  45.5 1.1 fusion.35
  48.4 0.9 pad_maximum_fusion.1
  49.3 3.9 %all-to-all-start.1 = ((f32[32,8,384]{2,1,0:T(8,128)}), f32[32,8,384]{2,1,0:T(8,128)S(1)}, u32[]{:S(2)}, u32[]{:S(2)}) async-start(f32[32,8,384]{2,1,0:T(8,128)} %pad_maximum_fusion.1), calls=%async_computation.1 | async-start | bytes 786432 | tf_op jit(solution)/shard_map/all_to_all | solution.py:284
  53.2 2.2 %collective-permute-start.1 = (s32[2,3]{1,0:T(2,128)S(1)}, s32[2,3]{1,0:T(2,128)S(1)}, u32[]{:S(2)}, u32[]{:S(2)}) collective-permute-start(s32[2,3]{1,0:T(2,128)S(1)} %copy-done.2), channel_id=1, source_target_pairs={{0,4},{1,5},{2,6},{3,7},{4,8},{5,9},{6,10},{7,11},{8,12},{9,13},{1... | collective-permute-start | bytes 80 | tf_op jit(solution)/shard_map/ppermute | solution.py:499
  55.4 3.6 %collective-permute-start = (s32[2,3]{1,0:T(2,128)S(1)}, s32[2,3]{1,0:T(2,128)S(1)}, u32[]{:S(2)}, u32[]{:S(2)}) collective-permute-start(s32[2,3]{1,0:T(2,128)S(1)} %copy-done.2), channel_id=1, source_target_pairs={{0,1},{1,2},{2,3},{4,5},{5,6},{6,7},{8,9},{9,10},{10,11},{12,13},{... | collective-permute-start | bytes 80 | tf_op jit(solution)/shard_map/ppermute | solution.py:499
  58.9 4.1 %collective-permute-start.2 = (s32[2,3]{1,0:T(2,128)S(1)}, s32[2,3]{1,0:T(2,128)S(1)}, u32[]{:S(2)}, u32[]{:S(2)}) collective-permute-start(s32[2,3]{1,0:T(2,128)S(1)} %copy-done.2), channel_id=1, source_target_pairs={{0,5},{1,6},{2,7},{4,9},{5,10},{6,11},{8,13},{9,14},{10,15},{12,17... | collective-permute-start | bytes 80 | tf_op jit(solution)/shard_map/ppermute | solution.py:499
  63.2 1.2 collective-permute-done.2
  65.0 0.9 copy.72
  65.9 15.6 %solve_back.1.field_ref = f32[64,128,256]{2,1,0:T(8,128)} custom-call(f32[64,128,256]{2,1,0:T(8,128)} %get-tuple-element.7.p_ref, f32[384,256]{1,0:T(8,128)} %bitcast.178, bf16[256,256]{1,0:T(8,128)(2,1)} %constant.28.clone.zh_ref, bf16[256,256]{1,0:T(8,128)(2,1)} %constant.29.clone.zl_ref, bf16[256,256]{1,0:T(8,128)(2,1)} %constant.72.clone.sy_ref, ...), custom_call_target="tpu_custom_call" | custom-call | tf_op jit(solution)/shard_map/solve_back/pallas_call | solution.py:287
  81.5 19.9 %cut_boxes.1 = f32[8,24,24,24]{3,2,1,0:T(8,128)} custom-call(s32[8,3]{1,0:T(8,128)} %add_subtract_fusion.corner_ref, f32[64,128,256]{2,1,0:T(8,128)} %solve_back.1.field_ref, f32[64,128,256]{2,1,0:T(8,128)} %other_ref.1), custom_call_target="tpu_custom_call" | custom-call | tf_op jit(solution)/shard_map/cut_boxes/pallas_call | solution.py:513
  101.5 1.8 %fusion.91 = (f32[2,24,24,24]{3,2,1,0:T(8,128)S(1)}, f32[2,24,24,24]{3,2,1,0:T(8,128)S(1)}, f32[2,24,24,24]{3,2,1,0:T(8,128)S(1)}, f32[2,24,24,24]{3,2,1,0:T(8,128)S(1)}) fusion(f32[8,24,24,24]{3,2,1,0:T(8,128)} %cut_boxes.1), kind=kLoop, calls=%fused_computation.224 | loop fusion | bytes 884736 | tf_op jit(solution)/shard_map/slice | solution.py:526
  103.9 1.3 collective-permute-start.4
  105.2 1.3 collective-permute-start.5
  106.5 1.5 collective-permute-start.3
  108.2 3.2 %collective-permute-done.5 = f32[2,24,576]{2,1,0:T(8,128)S(1)} collective-permute-done((f32[2,24,576]{2,1,0:T(8,128)S(1)}, f32[2,24,576]{2,1,0:T(8,128)S(1)}, u32[]{:S(2)}, u32[]{:S(2)}) %collective-permute-start.5) | collective-permute-done | bytes 110624 | tf_op jit(solution)/shard_map/ppermute | solution.py:499
  111.4 3.0 %collective-permute-done.3 = f32[2,24,576]{2,1,0:T(8,128)S(1)} collective-permute-done((f32[2,24,576]{2,1,0:T(8,128)S(1)}, f32[2,24,576]{2,1,0:T(8,128)S(1)}, u32[]{:S(2)}, u32[]{:S(2)}) %collective-permute-start.3) | collective-permute-done | bytes 110624 | tf_op jit(solution)/shard_map/ppermute | solution.py:499
  115.1 22.6 %filter_orbitals.1 = (f32[2,8,24,576]{3,2,1,0:T(8,128)}, f32[2,24,576]{2,1,0:T(8,128)}) custom-call(s32[2]{0:T(128)} %degree_ref.1, s32[2]{0:T(128)} %weight_ref.1, f32[2,24,576]{2,1,0:T(8,128)} %add_add_fusion.box_ref, f32[2,8,24,576]{3,2,1,0:T(8,128)} %orbital_ref.1), custom_call_target="tpu_custom_call" | custom-call | tf_op jit(solution)/shard_map/filter_orbitals/pallas_call | solution.py:529
  137.7 1.3 collective-permute-start.8
  139.0 6.3 %collective-permute-start.7 = (f32[2,24,576]{2,1,0:T(8,128)}, f32[2,24,576]{2,1,0:T(8,128)S(1)}, u32[]{:S(2)}, u32[]{:S(2)}) collective-permute-start(f32[2,24,576]{2,1,0:T(8,128)} %get-tuple-element.10), channel_id=1, source_target_pairs={{0,4},{1,5},{2,6},{3,7},{4,8},{5,9},{6,10},{7,11},{8,12},{9,13},{1... | collective-permute-start | bytes 331784 | tf_op jit(solution)/shard_map/ppermute | solution.py:499
  145.3 1.3 collective-permute-start.6
  146.7 3.3 %collective-permute-done.6 = f32[2,24,576]{2,1,0:T(8,128)S(1)} collective-permute-done((f32[2,24,576]{2,1,0:T(8,128)}, f32[2,24,576]{2,1,0:T(8,128)S(1)}, u32[]{:S(2)}, u32[]{:S(2)}) %collective-permute-start.6) | collective-permute-done | bytes 110624 | tf_op jit(solution)/shard_map/ppermute | solution.py:499
  150.0 0.9 pad_maximum_fusion
  150.9 0.9 reshape.182
  151.8 2.1 %pad.4.share_ref = f32[8,24,32,128]{3,2,1,0:T(8,128)} pad(f32[8,24,24,24]{3,2,1,0:T(8,128)S(1)} %reshape.182, f32[]{:T(128)} %constant.22.clone.1), padding=0_0x0_0x0_8x0_104 | pad | bytes 3588100 | tf_op jit(solution)/shard_map/jit(_pad)/pad | solution.py:557
  153.8 20.5 %patch_density.1 = f32[64,128,256]{2,1,0:T(8,128)} custom-call(s32[8,3]{1,0:T(8,128)} %add_subtract_fusion.corner_ref, f32[8,24,32,128]{3,2,1,0:T(8,128)} %pad.4.share_ref), custom_call_target="tpu_custom_call" | custom-call | tf_op jit(solution)/shard_map/patch_density/pallas_call | solution.py:559
  (67 shorter events, 6.9 us)
Async XLA Ops:
  0.6 40.8 %copy-start.1 = (f32[2,128]{1,0:T(2,128)S(1)}, f32[2,128]{1,0:T(2,128)}, u32[]{:S(2)}) copy-start(f32[2,128]{1,0:T(2,128)} %constant.90) | copy-start | bytes 3076
  0.6 42.4 %copy-start = (f32[512,512,1,1]{1,0,3,2:T(8,128)S(1)}, f32[512,512,1,1]{1,0,3,2:T(8,128)}, u32[]{:S(2)}) copy-start(f32[512,512,1,1]{1,0,3,2:T(8,128)} %constant.91) | copy-start | bytes 3145732
  21.6 19.1 %all-to-all-start = ((f32[32,8,384]{2,1,0:T(8,128)}), f32[32,8,384]{2,1,0:T(8,128)S(1)}, u32[]{:S(2)}, u32[]{:S(2)}) async-start(f32[32,8,384]{2,1,0:T(8,128)} %bitcast.1), calls=%async_computation | async-start | bytes 786432 | tf_op jit(solution)/shard_map/all_to_all | solution.py:241
  40.7 12.4 %copy-start.2 = (s32[2,3]{1,0:T(2,128)S(1)}, s32[2,3]{1,0:T(2,128)}, u32[]{:S(2)}) copy-start(s32[2,3]{1,0:T(2,128)} %param.21) | copy-start | bytes 76
  49.3 15.7 %all-to-all-start.1 = ((f32[32,8,384]{2,1,0:T(8,128)}), f32[32,8,384]{2,1,0:T(8,128)S(1)}, u32[]{:S(2)}, u32[]{:S(2)}) async-start(f32[32,8,384]{2,1,0:T(8,128)} %pad_maximum_fusion.1), calls=%async_computation.1 | async-start | bytes 786432 | tf_op jit(solution)/shard_map/all_to_all | solution.py:284
  53.2 10.0 %collective-permute-start.1 = (s32[2,3]{1,0:T(2,128)S(1)}, s32[2,3]{1,0:T(2,128)S(1)}, u32[]{:S(2)}, u32[]{:S(2)}) collective-permute-start(s32[2,3]{1,0:T(2,128)S(1)} %copy-done.2), channel_id=1, source_target_pairs={{0,4},{1,5},{2,6},{3,7},{4,8},{5,9},{6,10},{7,11},{8,12},{9,13},{1... | collective-permute-start | bytes 80 | tf_op jit(solution)/shard_map/ppermute | solution.py:499
  55.4 7.8 %collective-permute-start = (s32[2,3]{1,0:T(2,128)S(1)}, s32[2,3]{1,0:T(2,128)S(1)}, u32[]{:S(2)}, u32[]{:S(2)}) collective-permute-start(s32[2,3]{1,0:T(2,128)S(1)} %copy-done.2), channel_id=1, source_target_pairs={{0,1},{1,2},{2,3},{4,5},{5,6},{6,7},{8,9},{9,10},{10,11},{12,13},{... | collective-permute-start | bytes 80 | tf_op jit(solution)/shard_map/ppermute | solution.py:499
  58.9 5.4 %collective-permute-start.2 = (s32[2,3]{1,0:T(2,128)S(1)}, s32[2,3]{1,0:T(2,128)S(1)}, u32[]{:S(2)}, u32[]{:S(2)}) collective-permute-start(s32[2,3]{1,0:T(2,128)S(1)} %copy-done.2), channel_id=1, source_target_pairs={{0,5},{1,6},{2,7},{4,9},{5,10},{6,11},{8,13},{9,14},{10,15},{12,17... | collective-permute-start | bytes 80 | tf_op jit(solution)/shard_map/ppermute | solution.py:499
  103.9 4.3 %collective-permute-start.4 = (f32[2,24,576]{2,1,0:T(8,128)S(1)}, f32[2,24,576]{2,1,0:T(8,128)S(1)}, u32[]{:S(2)}, u32[]{:S(2)}) collective-permute-start(f32[2,24,576]{2,1,0:T(8,128)S(1)} %squeeze.31), channel_id=1, source_target_pairs={{4,0},{5,1},{6,2},{7,3},{8,4},{9,5},{10,6},{11,7},{12,8},{13,9},{1... | collective-permute-start | bytes 331784 | tf_op jit(solution)/shard_map/ppermute | solution.py:499
  105.2 6.2 %collective-permute-start.5 = (f32[2,24,576]{2,1,0:T(8,128)S(1)}, f32[2,24,576]{2,1,0:T(8,128)S(1)}, u32[]{:S(2)}, u32[]{:S(2)}) collective-permute-start(f32[2,24,576]{2,1,0:T(8,128)S(1)} %squeeze.32), channel_id=1, source_target_pairs={{5,0},{6,1},{7,2},{9,4},{10,5},{11,6},{13,8},{14,9},{15,10},{17,12... | collective-permute-start | bytes 331784 | tf_op jit(solution)/shard_map/ppermute | solution.py:499
  106.5 7.9 %collective-permute-start.3 = (f32[2,24,576]{2,1,0:T(8,128)S(1)}, f32[2,24,576]{2,1,0:T(8,128)S(1)}, u32[]{:S(2)}, u32[]{:S(2)}) collective-permute-start(f32[2,24,576]{2,1,0:T(8,128)S(1)} %squeeze.30), channel_id=1, source_target_pairs={{1,0},{2,1},{3,2},{5,4},{6,5},{7,6},{9,8},{10,9},{11,10},{13,12},{... | collective-permute-start | bytes 331784 | tf_op jit(solution)/shard_map/ppermute | solution.py:499
  137.7 8.9 %collective-permute-start.8 = (f32[2,24,576]{2,1,0:T(8,128)}, f32[2,24,576]{2,1,0:T(8,128)S(1)}, u32[]{:S(2)}, u32[]{:S(2)}) collective-permute-start(f32[2,24,576]{2,1,0:T(8,128)} %get-tuple-element.10), channel_id=1, source_target_pairs={{0,5},{1,6},{2,7},{4,9},{5,10},{6,11},{8,13},{9,14},{10,15},{12,17... | collective-permute-start | bytes 331784 | tf_op jit(solution)/shard_map/ppermute | solution.py:499
  139.0 7.6 %collective-permute-start.7 = (f32[2,24,576]{2,1,0:T(8,128)}, f32[2,24,576]{2,1,0:T(8,128)S(1)}, u32[]{:S(2)}, u32[]{:S(2)}) collective-permute-start(f32[2,24,576]{2,1,0:T(8,128)} %get-tuple-element.10), channel_id=1, source_target_pairs={{0,4},{1,5},{2,6},{3,7},{4,8},{5,9},{6,10},{7,11},{8,12},{9,13},{1... | collective-permute-start | bytes 331784 | tf_op jit(solution)/shard_map/ppermute | solution.py:499
  145.3 4.6 %collective-permute-start.6 = (f32[2,24,576]{2,1,0:T(8,128)}, f32[2,24,576]{2,1,0:T(8,128)S(1)}, u32[]{:S(2)}, u32[]{:S(2)}) collective-permute-start(f32[2,24,576]{2,1,0:T(8,128)} %get-tuple-element.10), channel_id=1, source_target_pairs={{0,1},{1,2},{2,3},{4,5},{5,6},{6,7},{8,9},{9,10},{10,11},{12,13},{... | collective-permute-start | bytes 331784 | tf_op jit(solution)/shard_map/ppermute | solution.py:499

commit v2 on v1

--- a/solution.py
+++ b/solution.py
@@ -99,7 +99,7 @@
                 right[row] += jnp.sum((last * u).reshape(part // 8, 8, depth), 0)
                 return u
 
-            u = lax.fori_loop(0, rows, back, jnp.zeros((part, depth), f32))
+            u = lax.fori_loop(0, rows, back, jnp.zeros((part, depth), f32), unroll=8)
             w_ref[pl.ds(2 * rows + cols + start, part), :] = u
         w_ref[pl.ds(0, rows), :] = jnp.sum(left[...], 1)
         w_ref[pl.ds(rows, rows), :] = jnp.sum(right[...], 1)
@@ -130,7 +130,8 @@
                 q[row, span, :] = p_ref[row, span, :] + p
                 return p
 
-            lax.fori_loop(0, rows, ahead, w_ref[pl.ds(2 * rows + start, part), :])
+            opening = w_ref[pl.ds(2 * rows + start, part), :]
+            lax.fori_loop(0, rows, ahead, opening, unroll=8)
         carry[...] = w_ref[pl.ds(2 * rows + cols, cols), :]
 
     base = (steps - 1 - step) * slabs
@@ -361,49 +362,111 @@
                 out_ref[index, k] = jnp.where(inside & here, value[:edge, :edge], 0.0)
                 return 0
 
-            lax.fori_loop(0, edge, one, 0)
+            lax.fori_loop(0, edge, one, 0, unroll=8)
+
+
+def to_blocks(value, edge, blocks):
+    lane = lax.broadcasted_iota(jnp.int32, (value.shape[0], 128), 1)
+    result = []
+    for block in range(blocks):
+        total = jnp.zeros((value.shape[0], 128), f32)
+        for group in range(128 // edge):
+            line = group * blocks + block
+            if line >= edge:
+                continue
+            source, offset = divmod(line * edge, 128)
+            target = group * edge
+            first = min(edge, 128 - offset)
+            for part, low, high in ((0, 0, first), (1, first, edge)):
+                if low < high:
+                    tile = value[:, (source + part) * 128 : (source + part + 1) * 128]
+                    tile = pltpu.roll(tile, (target - offset) % 128, 1)
+                    total = jnp.where((lane >= target + low) & (lane < target + high), tile, total)
+        result.append(total)
+    return result
+
+
+def from_blocks(values, edge, tiles):
+    blocks = len(values)
+    lane = lax.broadcasted_iota(jnp.int32, values[0].shape, 1)
+    result = []
+    for tile in range(tiles):
+        total = jnp.zeros(values[0].shape, f32)
+        for line in range(edge):
+            start = line * edge - tile * 128
+            if start >= 128 or start + edge <= 0:
+                continue
+            group, block = divmod(line, blocks)
+            moved = pltpu.roll(values[block], (start - group * edge) % 128, 1)
+            total = jnp.where((lane >= start) & (lane < start + edge), moved, total)
+        result.append(total)
+    return jnp.concatenate(result, 1)
 
 
 def filter_kernel(
-    degree_ref, weight_ref, box_ref, orbital_ref, out_ref, share_ref, state, slope_ref
+    degree_ref, weight_ref, box_ref, orbital_ref, out_ref, share_ref, state, slope_ref, flat
 ):
     which = pl.program_id(0)
     _, orbitals, edge, merged = orbital_ref.shape
-    lanes = state.shape[-1]
+    blocks = state.shape[2]
+    tiles = flat.shape[-1] // 128
     box = box_ref[0]
     low = jnp.min(box) + window_gap
     high = jnp.max(box) + kinetic_top
     centre = 0.5 * (high + low)
-    lane = lax.broadcasted_iota(jnp.int32, (orbitals, lanes), 1)
+    lane = lax.broadcasted_iota(jnp.int32, (orbitals, 128), 1)
     inner = lax.rem(lane, edge)
+    line = lax.div(lane, edge) * blocks
     not_low = inner != 0
     not_high = inner != edge - 1
-    inverse = 2.0 / (high - low + jnp.zeros((orbitals, lanes), f32))
-    hop = jnp.where(lane < merged, -inverse, 0.0)
+    used = lane < 128 // edge * edge
+    not_first = lane >= edge
+    not_last = lane < (128 // edge - 1) * edge
+    inverse = 2.0 / (high - low + jnp.zeros((orbitals, 128), f32))
+    hop = [jnp.where(used & (line + block < edge), -inverse, 0.0) for block in range(blocks)]
     state[...] = jnp.zeros_like(state)
-    slope_ref[...] = jnp.zeros_like(slope_ref)
-    state[0, 1 : edge + 1, :, :merged] = jnp.swapaxes(orbital_ref[0], 0, 1)
+    flat[...] = jnp.zeros_like(flat)
+    factor = 2.0 * inverse[:1, :1]
     for x in range(edge):
-        row = (3.0 - centre + box[x : x + 1]) * (2.0 * inverse[:1, :merged])
-        slope_ref[x, :, :merged] = jnp.broadcast_to(row, (orbitals, merged))
-
-    def image(source, x, before, current, after):
-        total = before + after
-        total = total + pltpu.roll(current, edge, 1) + pltpu.roll(current, lanes - edge, 1)
-        total = total + pltpu.roll(jnp.where(not_high, current, 0.0), 1, 1)
-        total = total + pltpu.roll(jnp.where(not_low, current, 0.0), lanes - 1, 1)
-        return slope_ref[x] * current + hop * total
+        row = (3.0 - centre + box[x : x + 1]) * factor
+        flat[x, :, :merged] = jnp.broadcast_to(row, (orbitals, merged))
+
+    def place_slope(x, _):
+        for block, value in enumerate(to_blocks(flat[x], edge, blocks)):
+            slope_ref[x, block] = value
+        return 0
+
+    lax.fori_loop(0, edge, place_slope, 0, unroll=4)
+    flat[:, :, :merged] = jnp.swapaxes(orbital_ref[0], 0, 1)
+
+    def place_state(x, _):
+        for block, value in enumerate(to_blocks(flat[x], edge, blocks)):
+            state[0, x + 1, block] = value
+        return 0
+
+    lax.fori_loop(0, edge, place_state, 0, unroll=4)
 
     def advance(source, target, opening):
-        before = state[source, 0]
-        current = state[source, 1]
+        before = [state[source, 0, block] for block in range(blocks)]
+        current = [state[source, 1, block] for block in range(blocks)]
         for x in range(edge):
-            after = state[source, x + 2]
-            value = image(source, x, before, current, after)
-            if opening:
-                state[target, x + 1] = 0.5 * value
-            else:
-                state[target, x + 1] = value - state[target, x + 1]
+            after = [state[source, x + 2, block] for block in range(blocks)]
+            wrapped_up = pltpu.roll(jnp.where(not_first, current[0], 0.0), 128 - edge, 1)
+            wrapped_down = pltpu.roll(jnp.where(not_last, current[-1], 0.0), edge, 1)
+            for block in range(blocks):
+                here = current[block]
+                up = current[block + 1] if block + 1 < blocks else wrapped_up
+                down = current[block - 1] if block > 0 else wrapped_down
+                total = (before[block] + after[block]) + (up + down)
+                total = total + (
+                    pltpu.roll(jnp.where(not_high, here, 0.0), 1, 1)
+                    + pltpu.roll(jnp.where(not_low, here, 0.0), 127, 1)
+                )
+                value = slope_ref[x, block] * here + hop[block] * total
+                if opening:
+                    state[target, x + 1, block] = 0.5 * value
+                else:
+                    state[target, x + 1, block] = value - state[target, x + 1, block]
             before, current = current, after
 
     degree = degree_ref[which]
@@ -425,19 +488,110 @@
         advance(1, 0, False)
 
     final = jnp.where(even, 0, 1)
-    squares = jnp.zeros((orbitals, lanes), f32)
+    squares = jnp.zeros((orbitals, 128), f32)
     for x in range(edge):
-        value = state[final, x + 1]
-        squares = squares + value * value
+        for block in range(blocks):
+            value = state[final, x + 1, block]
+            squares = squares + value * value
     total = jnp.sum(squares, axis=1, keepdims=True)
     scale = jnp.sqrt(edge**3 / (total + 1e-06))
     weight = weight_ref[which].astype(f32) / orbitals
-    for x in range(edge):
-        value = state[final, x + 1] * scale
-        state[final, x + 1] = value
+
+    def finish(x, _):
+        values = [state[final, x + 1, block] * scale for block in range(blocks)]
+        value = from_blocks(values, edge, tiles)
+        flat[x] = value
         share = weight * jnp.sum(value * value, axis=0, keepdims=True)
-        share_ref[0, x : x + 1] = share[:, :merged]
-    out_ref[0] = jnp.swapaxes(state[final, 1 : edge + 1], 0, 1)[:, :, :merged]
+        share_ref[0, pl.ds(x, 1), :] = share[:, :merged]
+        return 0
+
+    lax.fori_loop(0, edge, finish, 0, unroll=4)
+    out_ref[0] = jnp.swapaxes(flat[...], 0, 1)[:, :, :merged]
+
+
+def exchange_kernel(hops, peers, sign, in_ref, out_ref, slots, send_sems, recv_sems):
+    i = lax.axis_index("px")
+    j = lax.axis_index("py")
+
+    def exists(a, b):
+        return (i + a >= 0) & (i + a < peers[0]) & (j + b >= 0) & (j + b < peers[1])
+
+    barrier = pltpu.get_barrier_semaphore()
+    both_ways = [(a * s, b * s) for a, b in hops[1:] for s in (1, -1)]
+    for a, b in both_ways:
+
+        @pl.when(exists(a, b))
+        def _(a=a, b=b):
+            pl.semaphore_signal(
+                barrier, inc=1, device_id=(i + a, j + b), device_id_type=pl.DeviceIdType.MESH
+            )
+
+    pl.semaphore_wait(barrier, sum(exists(a, b).astype(jnp.int32) for a, b in both_ways))
+
+    def copy(index):
+        a, b = hops[index]
+        return pltpu.make_async_remote_copy(
+            src_ref=in_ref.at[index] if sign < 0 else in_ref,
+            dst_ref=slots.at[index - 1],
+            send_sem=send_sems.at[index - 1],
+            recv_sem=recv_sems.at[index - 1],
+            device_id=(i + sign * a, j + sign * b),
+            device_id_type=pl.DeviceIdType.MESH,
+        )
+
+    for index in range(1, len(hops)):
+
+        @pl.when(exists(sign * hops[index][0], sign * hops[index][1]))
+        def _(index=index):
+            copy(index).start()
+
+    if sign < 0:
+        out_ref[...] = in_ref[0]
+    else:
+        out_ref[0] = in_ref[...]
+    for index in range(1, len(hops)):
+        comes = exists(-sign * hops[index][0], -sign * hops[index][1])
+
+        @pl.when(comes)
+        def _(index=index):
+            copy(index).wait_recv()
+            if sign < 0:
+                out_ref[...] += slots[index - 1]
+            else:
+                out_ref[index] = slots[index - 1]
+
+        if sign > 0:
+
+            @pl.when(jnp.logical_not(comes))
+            def _(index=index):
+                out_ref[index] = jnp.zeros(out_ref.shape[1:], f32)
+
+    for index in range(1, len(hops)):
+
+        @pl.when(exists(sign * hops[index][0], sign * hops[index][1]))
+        def _(index=index):
+            copy(index).wait_send()
+
+
+def exchange(value, hops, peers, sign):
+    shape = value.shape[1:] if sign < 0 else value.shape
+    others = max(1, len(hops) - 1)
+    out_shape = shape if sign < 0 else (len(hops),) + shape
+    return pl.pallas_call(
+        functools.partial(exchange_kernel, hops, peers, sign),
+        in_specs=[pl.BlockSpec(memory_space=pltpu.VMEM)],
+        out_specs=pl.BlockSpec(memory_space=pltpu.VMEM),
+        out_shape=jax.ShapeDtypeStruct(out_shape, f32),
+        scratch_shapes=[
+            pltpu.VMEM((others,) + shape, f32),
+            pltpu.SemaphoreType.DMA((others,)),
+            pltpu.SemaphoreType.DMA((others,)),
+        ],
+        compiler_params=pltpu.CompilerParams(
+            vmem_limit_bytes=vmem_bytes, has_side_effects=True, collective_id=0 if sign < 0 else 1
+        ),
+        name="gather_boxes" if sign < 0 else "spread_shares",
+    )(value)
 
 
 def patch_kernel(edge, margin, corner_ref, share_ref, out_ref, total, sem):
@@ -445,7 +599,7 @@
     count, _, tall, lanes = share_ref.shape
 
     def clear(row, _):
-        total[row] = jnp.zeros(total.shape[1:], f32)
+        total[edge + row, margin : margin + cols] = jnp.zeros((cols, depth), f32)
         return 0
 
     lax.fori_loop(0, rows, clear, 0)
@@ -466,12 +620,12 @@
                     value = jnp.concatenate([value, jnp.zeros((tall, depth - lanes), f32)], 1)
                 value = pltpu.roll(value, turn, 0)
                 value = pltpu.roll(value, z, 1)
-                total[x + k, span, :] += value
+                total[edge + x + k, span, :] += value
                 return 0
 
-            lax.fori_loop(jnp.maximum(0, -x), jnp.minimum(edge, rows - x), one, 0)
-
-    copy = pltpu.make_async_copy(total.at[:, pl.ds(margin, cols), :], out_ref, sem)
+            lax.fori_loop(0, edge, one, 0, unroll=8)
+
+    copy = pltpu.make_async_copy(total.at[pl.ds(edge, rows), pl.ds(margin, cols), :], out_ref, sem)
     copy.start()
     copy.wait()
 
@@ -523,9 +677,10 @@
         name="cut_boxes",
     )(corners, field, external)
     pieces = pieces.reshape(len(hops), count, edge, merged)
-    boxes = sum(moved(pieces[index], -a, -b) for index, (a, b) in enumerate(hops))
-
-    lanes = -(-(merged + edge) // 128) * 128
+    boxes = exchange(pieces, hops, (peers_x, peers_y), -1)
+
+    lanes = -(-merged // 128) * 128
+    blocks = -(-edge // (128 // edge))
     filtered, shares = pl.pallas_call(
         filter_kernel,
         grid=(count,),
@@ -544,14 +699,15 @@
             jax.ShapeDtypeStruct((count, edge, merged), f32),
         ],
         scratch_shapes=[
-            pltpu.VMEM((2, edge + 2, orbital_count, lanes), f32),
+            pltpu.VMEM((2, edge + 2, blocks, orbital_count, 128), f32),
+            pltpu.VMEM((edge, blocks, orbital_count, 128), f32),
             pltpu.VMEM((edge, orbital_count, lanes), f32),
         ],
         compiler_params=params(),
         name="filter_orbitals",
     )(degrees, weights, boxes, orbitals)
 
-    parts = jnp.concatenate([moved(shares, a, b) for a, b in hops], 0)
+    parts = exchange(shares, hops, (peers_x, peers_y), 1)
     parts = parts.reshape(total, edge, edge, edge)
     side = min(128, depth)
     parts = jnp.pad(parts, ((0, 0), (0, 0), (0, tall - edge), (0, side - edge)))
@@ -562,7 +718,7 @@
         out_specs=anywhere,
         out_shape=jax.ShapeDtypeStruct(density.shape, f32),
         scratch_shapes=[
-            pltpu.VMEM((rows, cols + 2 * margin, depth), f32),
+            pltpu.VMEM((rows + 2 * edge, cols + 2 * margin, depth), f32),
             pltpu.SemaphoreType.DMA,
         ],
         compiler_params=params(),

time: 174 us -> 146 us (0.84)
  starting transfers between devices: 34 us -> 21 us
  waiting for transfers between devices: 21.8 us -> 12.2 us
  Pallas kernels: 97.7 us -> 91.6 us
    pallas_call x0 -> x2, Pallas kernels: none -> 24.6 us  [exchange(): pl.pallas_call(functools.partial(exchange_kernel, hops, peers, sign), in_...]
    ppermute x9 -> x3, starting transfers between devices: 22.8 us -> 9.86 us  [moved(): return lax.ppermute(value, ('px', 'py'), pairs)]
    pallas_call x1, Pallas kernels: 20.5 us -> 8.66 us  [body(): pl.pallas_call(functools.partial(patch_kernel, edge, margin), in_specs=[s...]
    pallas_call x1, Pallas kernels: 19.9 us -> 8.34 us  [body(): pl.pallas_call(functools.partial(cut_kernel, edge), in_specs=[scalars, an...]
    ppermute x9 -> x3, waiting for transfers between devices: 10.7 us -> 1.2 us  [moved(): return lax.ppermute(value, ('px', 'py'), pairs)]
    pallas_call x1, Pallas kernels: 22.6 us -> 17.6 us  [body(): pl.pallas_call(filter_kernel, grid=(count,), in_specs=[scalars, scalars,...]
    reshape x0 -> x1, local copies, waits for them, and re-layouts: none -> 2.9 us  [body(): pieces = pieces.reshape(len(hops), count, edge, merged)]
    slice x1 -> x0, local copies, waits for them, and re-layouts: 1.77 us -> none  [body(): pieces[index]]
  transfers between devices with their start and end apart: 11 -> 5, of which waited for: 5 -> 2; matrix products, arithmetic and copies ran while one was open for 1% -> 1% of each run, Pallas kernels for 0% -> 0%
where the time goes in v2:
time: 146 us
  Pallas kernels  91.6 us (63%)
  starting transfers between devices  21 us (14%)
  waiting for transfers between devices  12.2 us (8%)
  local copies, waits for them, and re-layouts  10.6 us (7%)
  other arithmetic  4.48 us (3%)
  matrix products  4.41 us (3%)
    pallas_call x2, Pallas kernels, exchange(): pl.pallas_call(functools.partial(exchange_kernel, hops, peers, sign), in_...  24.6 us
    pallas_call x1, Pallas kernels, hartree(): pl.pallas_call(forward_kernel, grid=(steps,), in_specs=[pl.BlockSpec((sla...  17.7 us
    pallas_call x1, Pallas kernels, body(): pl.pallas_call(filter_kernel, grid=(count,), in_specs=[scalars, scalars,...  17.6 us
    pallas_call x1, Pallas kernels, hartree(): pl.pallas_call(backward_kernel, grid=(steps,), in_specs=[whole((rows, col...  14.7 us
    all_to_all x1, waiting for transfers between devices, hartree(): lax.all_to_all(sent, ('px', 'py'), split_axis=0, concat_axis=0, tiled=True)  11 us
    ppermute x3, starting transfers between devices, moved(): return lax.ppermute(value, ('px', 'py'), pairs)  9.86 us
    pallas_call x1, Pallas kernels, body(): pl.pallas_call(functools.partial(patch_kernel, edge, margin), in_specs=[s...  8.66 us
    pallas_call x1, Pallas kernels, body(): pl.pallas_call(functools.partial(cut_kernel, edge), in_specs=[scalars, an...  8.34 us
  transfers between devices with their start and end apart: 5, of which 2 were waited for; matrix products, arithmetic and copies ran while one was open for 1% of the time, Pallas kernels for 0%

profile of v2, /device:TPU:0, one launch (start us, length us, event | category | flops | bytes accessed | tf_op | source)
XLA Modules:
  0.0 145.5 jit_solution(16526821917957699611)
XLA Ops:
  0.7 17.7 %solve_ahead.1 = (f32[64,128,256]{2,1,0:T(8,128)}, f32[384,256]{1,0:T(8,128)}) custom-call(f32[64,128,256]{2,1,0:T(8,128)} %x_ref.1, bf16[256,256]{1,0:T(8,128)(2,1)} %constant.28.clone.zh_ref, bf16[256,256]{1,0:T(8,128)(2,1)} %constant.29.clone.zl_ref, bf16[256,256]{1,0:T(8,128)(2,1)} %constant.72.clone.sy_ref, f32[128,256]{1,0:T(8,128)} %constant.73.clone.r_ref, ...), custom_call_target="tpu_custom_call" | custom-call | tf_op jit(solution)/shard_map/solve_ahead/pallas_call | solution.py:183
  18.3 1.9 %copy.61 = f32[256,384]{1,0:T(8,128)} copy(f32[256,384]{0,1:T(8,128)} %bitcast.178) | data formatting | bytes 786432 | tf_op jit(solution)/shard_map/transpose | solution.py:241
  20.2 7.3 %all-to-all-start = ((f32[32,8,384]{2,1,0:T(8,128)}), f32[32,8,384]{2,1,0:T(8,128)S(1)}, u32[]{:S(2)}, u32[]{:S(2)}) async-start(f32[32,8,384]{2,1,0:T(8,128)} %bitcast.1), calls=%async_computation | async-start | bytes 786432 | tf_op jit(solution)/shard_map/all_to_all | solution.py:242
  27.6 0.7 dynamic-slice_negate_fusion
  28.3 11.0 %all-to-all-done = f32[32,8,384]{2,1,0:T(8,128)S(1)} async-done(((f32[32,8,384]{2,1,0:T(8,128)}), f32[32,8,384]{2,1,0:T(8,128)S(1)}, u32[]{:S(2)}, u32[]{:S(2)}) %all-to-all-start) | async-done | bytes 393248 | tf_op jit(solution)/shard_map/all_to_all | solution.py:242
  39.9 0.2 copy_bitcast_fusion.1
  40.1 0.8 fusion.4
  40.8 0.6 fusion.3
  41.6 0.8 fusion.33
  42.5 0.8 fusion.56
  43.3 0.8 add_bitcast_fusion.2
  44.1 1.1 fusion.35
  45.4 0.6 fusion.5
  46.0 0.5 fusion.6
  46.5 0.2 slice_add_fusion
  47.0 0.9 pad_maximum_fusion
  47.9 3.9 %all-to-all-start.1 = ((f32[32,8,384]{2,1,0:T(8,128)}), f32[32,8,384]{2,1,0:T(8,128)S(1)}, u32[]{:S(2)}, u32[]{:S(2)}) async-start(f32[32,8,384]{2,1,0:T(8,128)} %pad_maximum_fusion), calls=%async_computation.1 | async-start | bytes 786432 | tf_op jit(solution)/shard_map/all_to_all | solution.py:285
  51.8 2.2 %collective-permute-start.1 = (s32[2,3]{1,0:T(2,128)S(1)}, s32[2,3]{1,0:T(2,128)S(1)}, u32[]{:S(2)}, u32[]{:S(2)}) collective-permute-start(s32[2,3]{1,0:T(2,128)S(1)} %copy-done.2), channel_id=1, source_target_pairs={{0,4},{1,5},{2,6},{3,7},{4,8},{5,9},{6,10},{7,11},{8,12},{9,13},{1... | collective-permute-start | bytes 80 | tf_op jit(solution)/shard_map/ppermute | solution.py:653
  54.0 3.6 %collective-permute-start = (s32[2,3]{1,0:T(2,128)S(1)}, s32[2,3]{1,0:T(2,128)S(1)}, u32[]{:S(2)}, u32[]{:S(2)}) collective-permute-start(s32[2,3]{1,0:T(2,128)S(1)} %copy-done.2), channel_id=1, source_target_pairs={{0,1},{1,2},{2,3},{4,5},{5,6},{6,7},{8,9},{9,10},{10,11},{12,13},{... | collective-permute-start | bytes 80 | tf_op jit(solution)/shard_map/ppermute | solution.py:653
  57.5 4.1 %collective-permute-start.2 = (s32[2,3]{1,0:T(2,128)S(1)}, s32[2,3]{1,0:T(2,128)S(1)}, u32[]{:S(2)}, u32[]{:S(2)}) collective-permute-start(s32[2,3]{1,0:T(2,128)S(1)} %copy-done.2), channel_id=1, source_target_pairs={{0,5},{1,6},{2,7},{4,9},{5,10},{6,11},{8,13},{9,14},{10,15},{12,17... | collective-permute-start | bytes 80 | tf_op jit(solution)/shard_map/ppermute | solution.py:653
  61.8 1.2 collective-permute-done.2
  63.0 0.6 add_subtract_fusion.corner_ref
  63.6 0.9 copy.72
  64.5 14.7 %solve_back.1.field_ref = f32[64,128,256]{2,1,0:T(8,128)} custom-call(f32[64,128,256]{2,1,0:T(8,128)} %get-tuple-element.7.p_ref, f32[384,256]{1,0:T(8,128)} %bitcast.174, bf16[256,256]{1,0:T(8,128)(2,1)} %constant.28.clone.zh_ref, bf16[256,256]{1,0:T(8,128)(2,1)} %constant.29.clone.zl_ref, bf16[256,256]{1,0:T(8,128)(2,1)} %constant.72.clone.sy_ref, ...), custom_call_target="tpu_custom_call" | custom-call | tf_op jit(solution)/shard_map/solve_back/pallas_call | solution.py:288
  79.2 8.3 %cut_boxes.1 = f32[8,24,24,24]{3,2,1,0:T(8,128)} custom-call(s32[8,3]{1,0:T(8,128)} %add_subtract_fusion.corner_ref, f32[64,128,256]{2,1,0:T(8,128)} %solve_back.1.field_ref, f32[64,128,256]{2,1,0:T(8,128)} %other_ref.1), custom_call_target="tpu_custom_call" | custom-call | tf_op jit(solution)/shard_map/cut_boxes/pallas_call | solution.py:667
  87.5 2.9 %reshape.176.in_ref = f32[4,2,24,576]{3,2,1,0:T(8,128)} reshape(f32[8,24,24,24]{3,2,1,0:T(8,128)} %cut_boxes.1) | data formatting | bytes 884736 | tf_op jit(solution)/shard_map/reshape | solution.py:679
  90.4 8.9 %gather_boxes.1.box_ref = f32[2,24,576]{2,1,0:T(8,128)} custom-call(f32[4,2,24,576]{3,2,1,0:T(8,128)} %reshape.176.in_ref), custom_call_target="tpu_custom_call" | custom-call | tf_op jit(solution)/shard_map/gather_boxes/pallas_call | solution.py:580
  99.3 17.6 %filter_orbitals.1 = (f32[2,8,24,576]{3,2,1,0:T(8,128)}, f32[2,24,576]{2,1,0:T(8,128)}) custom-call(s32[2]{0:T(128)} %degree_ref.1, s32[2]{0:T(128)} %weight_ref.1, f32[2,24,576]{2,1,0:T(8,128)} %gather_boxes.1.box_ref, f32[2,8,24,576]{3,2,1,0:T(8,128)} %orbital_ref.1), custom_call_target="tpu_custom_call" | custom-call | tf_op jit(solution)/shard_map/filter_orbitals/pallas_call | solution.py:684
  117.0 15.7 %spread_shares.1 = f32[4,2,24,576]{3,2,1,0:T(8,128)} custom-call(f32[2,24,576]{2,1,0:T(8,128)} %get-tuple-element.10.in_ref), custom_call_target="tpu_custom_call" | custom-call | tf_op jit(solution)/shard_map/spread_shares/pallas_call | solution.py:580
  132.7 2.0 %reshape.177 = f32[8,24,24,24]{3,2,1,0:T(8,128)S(1)} reshape(f32[4,2,24,576]{3,2,1,0:T(8,128)} %spread_shares.1) | data formatting | bytes 884736 | tf_op jit(solution)/shard_map/reshape | solution.py:711
  134.6 2.1 %pad.4.share_ref = f32[8,24,32,128]{3,2,1,0:T(8,128)} pad(f32[8,24,24,24]{3,2,1,0:T(8,128)S(1)} %reshape.177, f32[]{:T(128)} %constant.22.clone.1), padding=0_0x0_0x0_8x0_104 | pad | bytes 3588100 | tf_op jit(solution)/shard_map/jit(_pad)/pad | solution.py:713
  136.7 8.7 %patch_density.1 = f32[64,128,256]{2,1,0:T(8,128)} custom-call(s32[8,3]{1,0:T(8,128)} %add_subtract_fusion.corner_ref, f32[8,24,32,128]{3,2,1,0:T(8,128)} %pad.4.share_ref), custom_call_target="tpu_custom_call" | custom-call | tf_op jit(solution)/shard_map/patch_density/pallas_call | solution.py:715
  (51 shorter events, 1.3 us)
Async XLA Ops:
  0.6 39.4 %copy-start.1 = (f32[2,128]{1,0:T(2,128)S(1)}, f32[2,128]{1,0:T(2,128)}, u32[]{:S(2)}) copy-start(f32[2,128]{1,0:T(2,128)} %constant.90) | copy-start | bytes 3076
  0.6 41.0 %copy-start = (f32[512,512,1,1]{1,0,3,2:T(8,128)S(1)}, f32[512,512,1,1]{1,0,3,2:T(8,128)}, u32[]{:S(2)}) copy-start(f32[512,512,1,1]{1,0,3,2:T(8,128)} %constant.91) | copy-start | bytes 3145732
  20.2 19.1 %all-to-all-start = ((f32[32,8,384]{2,1,0:T(8,128)}), f32[32,8,384]{2,1,0:T(8,128)S(1)}, u32[]{:S(2)}, u32[]{:S(2)}) async-start(f32[32,8,384]{2,1,0:T(8,128)} %bitcast.1), calls=%async_computation | async-start | bytes 786432 | tf_op jit(solution)/shard_map/all_to_all | solution.py:242
  39.3 12.4 %copy-start.2 = (s32[2,3]{1,0:T(2,128)S(1)}, s32[2,3]{1,0:T(2,128)}, u32[]{:S(2)}) copy-start(s32[2,3]{1,0:T(2,128)} %param.21) | copy-start | bytes 76
  47.9 15.7 %all-to-all-start.1 = ((f32[32,8,384]{2,1,0:T(8,128)}), f32[32,8,384]{2,1,0:T(8,128)S(1)}, u32[]{:S(2)}, u32[]{:S(2)}) async-start(f32[32,8,384]{2,1,0:T(8,128)} %pad_maximum_fusion), calls=%async_computation.1 | async-start | bytes 786432 | tf_op jit(solution)/shard_map/all_to_all | solution.py:285
  51.8 10.0 %collective-permute-start.1 = (s32[2,3]{1,0:T(2,128)S(1)}, s32[2,3]{1,0:T(2,128)S(1)}, u32[]{:S(2)}, u32[]{:S(2)}) collective-permute-start(s32[2,3]{1,0:T(2,128)S(1)} %copy-done.2), channel_id=1, source_target_pairs={{0,4},{1,5},{2,6},{3,7},{4,8},{5,9},{6,10},{7,11},{8,12},{9,13},{1... | collective-permute-start | bytes 80 | tf_op jit(solution)/shard_map/ppermute | solution.py:653
  54.0 7.8 %collective-permute-start = (s32[2,3]{1,0:T(2,128)S(1)}, s32[2,3]{1,0:T(2,128)S(1)}, u32[]{:S(2)}, u32[]{:S(2)}) collective-permute-start(s32[2,3]{1,0:T(2,128)S(1)} %copy-done.2), channel_id=1, source_target_pairs={{0,1},{1,2},{2,3},{4,5},{5,6},{6,7},{8,9},{9,10},{10,11},{12,13},{... | collective-permute-start | bytes 80 | tf_op jit(solution)/shard_map/ppermute | solution.py:653
  57.5 5.4 %collective-permute-start.2 = (s32[2,3]{1,0:T(2,128)S(1)}, s32[2,3]{1,0:T(2,128)S(1)}, u32[]{:S(2)}, u32[]{:S(2)}) collective-permute-start(s32[2,3]{1,0:T(2,128)S(1)} %copy-done.2), channel_id=1, source_target_pairs={{0,5},{1,6},{2,7},{4,9},{5,10},{6,11},{8,13},{9,14},{10,15},{12,17... | collective-permute-start | bytes 80 | tf_op jit(solution)/shard_map/ppermute | solution.py:653
